TPU v7x, 128 devices: a whole 4x4x4 slice. The times are simulated.
128 devices in a mesh: ctx: 64 (over x, y, z_hi, core), head: 2 (over z_lo).
Axes of the slice: x: 4, y: 4, z: 4 (z_hi: 2, z_lo: 2; z = z_hi * 2 + z_lo), core: 2. Of those that a mesh axis runs over, the one named last changes fastest.
Arguments:
- content_rows: bfloat16 [4, 512, 4, 2048], P(None, 'ctx'), may hold values from -6 to 6
- w_hidden: bfloat16 [2048, 4096], P(None, 'head'), may hold values from -0.125 to 0.125
- w_embed: bfloat16 [4096, 512], P('head'), may hold values from -0.09375 to 0.09375
- w_query: bfloat16 [512, 512], P(None, 'head'), may hold values from -0.25 to 0.25
- w_gate: bfloat16 [512, 512], P(None, 'head'), may hold values from -0.25 to 0.25
- w_proj: bfloat16 [512, 512], P('head'), may hold values from -0.25 to 0.25
- history_keys: bfloat16 [4, 147456, 512], P(None, 'ctx', 'head'), may hold values from -6 to 6
- history_values: bfloat16 [4, 147456, 512], P(None, 'ctx', 'head'), may hold values from -6 to 6
- cutoffs: int32 [4, 512], replicated, may hold values from 36864 to 147456
- out_cotangent: bfloat16 [4, 512, 512], P(None, 'ctx'), may hold values from -6 to 6
Outputs:
- content_grad: bfloat16 [4, 512, 4, 2048], P(None, 'ctx', 'head')
Inputs may be any that keep to these rules, and one draw needn't show every extreme that they name: cutoffs[u, t] counts the leading events of user u's history that its target t sees.
All inputs are finite; a program needn't handle non-finite values.
Results may differ from a plain program's by a relative error of at most 0.02.
Values may be sent and summed in bfloat16 or wider, within the bound.
A program may use at most 128 MiB of HBM per device.

v0:
```python
import jax
import jax.numpy as jnp
from jax import lax
from jax.sharding import Mesh
from jax.sharding import PartitionSpec as P

DH = 128
CTX = ("ctx_0", "ctx_1", "ctx_2", "ctx_3")


def from_everyone(shard, axis):
    copies = jnp.broadcast_to(shard, (lax.axis_size(axis), *shard.shape))
    return lax.all_to_all(copies, axis, split_axis=0, concat_axis=0, tiled=True)


def of_everyone(shard, axis):
    return from_everyone(shard, axis).sum(axis=0)


def in_order(blocks, dim):
    blocks = jnp.moveaxis(blocks, 0, dim)
    shape = blocks.shape
    return blocks.reshape(*shape[:dim], shape[dim] * shape[dim + 1], *shape[dim + 2 :])


def gather_axes(shard, axes, dim):
    far, near = axes
    blocks = from_everyone(from_everyone(shard, far), near)
    return in_order(blocks.swapaxes(0, 1).reshape(-1, *shard.shape), dim)


def side_by_side(arrays, axis, dim, along):
    ends, at = ([], 0)
    for a in arrays[:-1]:
        at += a.shape[along]
        ends.append(at)
    both = jnp.concatenate(arrays, axis=along)
    return tuple(jnp.split(gather_axes(both, axis, dim), ends, axis=along))


def cut_along(shard, dim, size):
    before, after = (shard.shape[:dim], shard.shape[dim + 1 :])
    return jnp.moveaxis(shard.reshape(*before, size, -1, *after), dim, 0)


def sent_and_summed(shard, axis, dim):
    size = lax.axis_size(axis)
    blocks = lax.all_to_all(cut_along(shard, dim, size), axis, 0, 0, tiled=True)
    return jnp.sum(blocks.astype(jnp.float32), axis=0)


def summed_rows_2(shard, axes, dim):
    far, near = axes
    blocks = cut_along(shard, dim, lax.axis_size(far))
    nearer = sent_and_summed(blocks, near, dim + 1)
    arrived = lax.all_to_all(
        nearer.astype(jnp.bfloat16), far, split_axis=0, concat_axis=0, tiled=True
    )
    return arrived.astype(jnp.float32).sum(axis=0)


def padded_to(lines, size):
    spare = -len(lines) % size
    return jnp.pad(lines, [(0, spare)] + [(0, 0)] * (lines.ndim - 1))


def sum_by_parts(shard, axes):
    lines = shard.reshape(-1, shard.shape[-1])
    own = summed_rows_2(padded_to(lines, lax.axis_size(axes[0]) * lax.axis_size(axes[1])), axes, 0)
    whole = gather_axes(own.astype(jnp.bfloat16), axes, 0)
    return whole[: len(lines)].reshape(shard.shape).astype(jnp.float32)


def taken_together(shard, axis):
    everything = from_everyone(shard, axis)
    return jnp.sum(everything.astype(jnp.float32), axis=0)


def silu_slope(values_in):
    sigmoid_part = jax.nn.sigmoid(values_in)
    return sigmoid_part * (1.0 + values_in * (1.0 - sigmoid_part))


def contract_last(left, right):
    return lax.dot_general(
        left, right, (((1,), (1,)), ((), ())), preferred_element_type=jnp.float32
    )


def norm_grads(attended, gates, out_grad, heads_here):
    lead = attended.shape[:-1]
    attn_heads = attended.reshape(lead + (heads_here, DH))
    rscale = lax.rsqrt(jnp.mean(attn_heads * attn_heads, axis=-1, keepdims=True) + 1e-06)
    normed = attn_heads * rscale
    grad_heads = out_grad.reshape(lead + (heads_here, DH)).astype(jnp.float32)
    gate_heads = gates.reshape(lead + (heads_here, DH)).astype(jnp.float32)
    gate_grad = (grad_heads * normed).reshape(attended.shape)
    normed_grad = grad_heads * gate_heads
    attn_grad = rscale * (
        normed_grad - normed * jnp.mean(normed_grad * normed, axis=-1, keepdims=True)
    )
    return (attn_grad.reshape(attended.shape).astype(jnp.bfloat16), gate_grad)


def body(
    content_rows,
    w_hidden,
    w_embed,
    w_query,
    w_gate,
    w_proj,
    history_keys,
    history_values,
    cutoffs,
    out_cotangent,
):
    user_count, shard_rows, rows_each, width_in = content_rows.shape
    half_hidden = w_hidden.shape[1]
    model_width = w_query.shape[0]
    local_width = w_query.shape[1]
    heads_here = local_width // DH
    events = history_keys.shape[1]
    target_rows = user_count * shard_rows
    hidden_lin = jnp.dot(
        content_rows.reshape(-1, width_in), w_hidden, preferred_element_type=jnp.float32
    )
    hidden = jax.nn.silu(hidden_lin).astype(jnp.bfloat16)
    encoded = jnp.dot(hidden, w_embed, preferred_element_type=jnp.float32)
    summed = of_everyone(
        jnp.sum(encoded.reshape(target_rows, rows_each, model_width), axis=1), "head"
    )
    embedded = (0.5 * summed).astype(jnp.bfloat16)
    query_lin = jnp.dot(embedded, w_query, preferred_element_type=jnp.float32)
    gate_lin = jnp.dot(embedded, w_gate, preferred_element_type=jnp.float32)
    queries = (
        jax.nn.silu(query_lin).astype(jnp.bfloat16).reshape(user_count, shard_rows, local_width)
    )
    gates = jax.nn.silu(gate_lin).astype(jnp.bfloat16).reshape(user_count, shard_rows, local_width)
    out_grad = contract_last(out_cotangent.reshape(-1, model_width), w_proj).astype(jnp.bfloat16)
    out_grad = out_grad.reshape(user_count, shard_rows, local_width)
    score_scale = DH ** (-0.5)
    positions = lax.axis_index(CTX) * events + jnp.arange(events, dtype=jnp.int32)
    key_heads = history_keys.reshape(user_count, events, heads_here, DH)
    value_heads = history_values.reshape(user_count, events, heads_here, DH)

    def forward_user(packed):
        user_queries, limits, user_keys, user_values = packed
        row_count = user_queries.shape[0]
        scores = (
            jnp.einsum(
                "thd,phd->htp",
                user_queries.reshape(row_count, heads_here, DH),
                user_keys,
                preferred_element_type=jnp.float32,
            )
            * score_scale
        )
        visible = positions[None, :] < limits[:, None]
        weights = jnp.where(visible[None], jax.nn.silu(scores), 0.0).astype(jnp.bfloat16)
        summed_rows = jnp.einsum(
            "htp,phd->thd", weights, user_values, preferred_element_type=jnp.float32
        )
        return summed_rows.reshape(row_count, local_width)

    queries_all, gates_all, out_grad_all = side_by_side(
        (queries, gates, out_grad), (("ctx_0", "ctx_1", "ctx_2"), "ctx_3"), 1, 0
    )
    partial_value = lax.map(forward_user, (queries_all, cutoffs, key_heads, value_heads))
    attended_all = sum_by_parts(
        partial_value.astype(jnp.bfloat16), (("ctx_0", "ctx_1", "ctx_2"), "ctx_3")
    )
    grads_all, gate_grad_all = norm_grads(attended_all, gates_all, out_grad_all, heads_here)
    gate_grad = lax.dynamic_slice_in_dim(
        gate_grad_all, lax.axis_index(CTX) * shard_rows, shard_rows, 1
    )

    def backward_user(packed):
        user_queries, limits, user_keys, user_values, user_grads = packed
        row_count = user_queries.shape[0]
        scores = (
            jnp.einsum(
                "thd,phd->htp",
                user_queries.reshape(row_count, heads_here, DH),
                user_keys,
                preferred_element_type=jnp.float32,
            )
            * score_scale
        )
        visible = positions[None, :] < limits[:, None]
        weight_grad = jnp.einsum(
            "thd,phd->htp",
            user_grads.reshape(row_count, heads_here, DH),
            user_values,
            preferred_element_type=jnp.float32,
        )
        grad_scores = jnp.where(visible[None], weight_grad * silu_slope(scores), 0.0).astype(
            jnp.bfloat16
        )
        summed_rows = jnp.einsum(
            "htp,phd->thd", grad_scores, user_keys, preferred_element_type=jnp.float32
        )
        return summed_rows.reshape(row_count, local_width) * score_scale

    query_partial = lax.map(
        backward_user, (queries_all, cutoffs, key_heads, value_heads, grads_all)
    )
    query_grad = summed_rows_2(
        query_partial.astype(jnp.bfloat16), (("ctx_0", "ctx_1", "ctx_2"), "ctx_3"), 1
    )
    query_back = (query_grad.reshape(-1, local_width) * silu_slope(query_lin)).astype(jnp.bfloat16)
    gate_back = (gate_grad.reshape(-1, local_width) * silu_slope(gate_lin)).astype(jnp.bfloat16)
    embed_part = contract_last(query_back, w_query) + contract_last(gate_back, w_gate)
    embed_grad = (
        0.5 * taken_together(embed_part.astype(jnp.bfloat16), "head").astype(jnp.float32)
    ).astype(jnp.bfloat16)
    hidden_grad = contract_last(embed_grad, w_embed)
    slopes = silu_slope(hidden_lin).reshape(target_rows, rows_each, half_hidden)
    hidden_back = (hidden_grad[:, None, :] * slopes).astype(jnp.bfloat16).reshape(-1, half_hidden)
    content_part = contract_last(hidden_back, w_hidden).reshape(
        user_count, shard_rows, rows_each, width_in
    )
    return sent_and_summed(content_part.astype(jnp.bfloat16), "head", 2).astype(jnp.bfloat16)


def solution(mesh):
    split = Mesh(
        mesh.devices.reshape(4, 4, 2, 2, mesh.shape["head"]),
        ("ctx_0", "ctx_1", "ctx_2", "ctx_3", "head"),
    )
    return jax.shard_map(
        body,
        mesh=split,
        in_specs=(
            P(None, CTX, None, None),
            P(None, "head"),
            P("head", None),
            P(None, "head"),
            P(None, "head"),
            P("head", None),
            P(None, CTX, "head"),
            P(None, CTX, "head"),
            P(),
            P(None, CTX, None),
        ),
        out_specs=P(None, CTX, "head", None),
        check_vma=False,
    )
```

profile of v0, /device:TPU:0, one launch (start us, length us, event | category | flops | bytes accessed | tf_op | source)
XLA Modules:
  0.0 359.8 jit_solution(17615038172251934614)
XLA Ops:
  0.0 1.3 reshape.183
  1.3 4.6 %fusion.69 = f32[128,2048]{1,0:T(8,128)S(1)} fusion(bf16[128,2048]{1,0:T(8,128)(2,1)S(1)} %reshape.183, bf16[2048,2048]{1,0:T(8,128)(2,1)} %param.15), kind=kOutput, calls=%fused_computation.96 | convolution fusion | flops 1073741824 | bytes 9961472 | tf_op jit(solution)/shard_map/dot_general | solution.py:124
  8.4 3.4 all-to-all-start
  12.0 4.3 %all-to-all-done = f32[2,32,512]{2,1,0:T(8,128)S(1)} async-done(((f32[2,32,512]{2,1,0:T(8,128)}), f32[2,32,512]{2,1,0:T(8,128)S(1)}, u32[]{:S(2)}, u32[]{:S(2)}) %all-to-all-start) | async-done | bytes 131104 | tf_op jit(solution)/shard_map/all_to_all | solution.py:13
  16.7 1.3 broadcast_in_dim.53
  18.0 10.8 %all-to-all-start.1 = ((bf16[32,12,8,256]{3,2,1,0:T(8,128)(2,1)}), bf16[32,12,8,256]{3,2,1,0:T(8,128)(2,1)}, u32[]{:S(2)}, u32[]{:S(2)}) async-start(bf16[32,12,8,256]{3,2,1,0:T(8,128)(2,1)} %broadcast_in_dim.53), calls=%async_computation.1 | async-start | bytes 3145728 | tf_op jit(solution)/shard_map/all_to_all | solution.py:13
  28.8 6.8 %copy.108 = bf16[4,2304,256]{1,2,0:T(8,128)(2,1)} copy(bf16[4,2304,256]{2,1,0:T(8,128)(2,1)} %param.20) | data formatting | bytes 9437184 | tf_op args[6]
  35.7 6.6 %copy.117 = bf16[4,2304,2,128]{3,1,2,0:T(8,128)(2,1)} copy(bf16[4,2304,2,128]{1,3,2,0:T(8,128)(2,1)} %bitcast.145) | data formatting | bytes 9437184
  42.3 6.7 %copy.109 = bf16[4,2304,256]{1,2,0:T(8,128)(2,1)} copy(bf16[4,2304,256]{2,1,0:T(8,128)(2,1)} %param.21) | data formatting | bytes 9437184 | tf_op args[7]
  49.0 3.1 all-to-all-done.1
  52.1 1.5 copy.110
  54.0 6.3 %all_to_all.55 = bf16[2,32,12,8,256]{4,3,1,2,0:T(8,128)(2,1)S(1)} all-to-all(bf16[2,32,12,8,256]{4,3,1,2,0:T(8,128)(2,1)S(1)} %broadcast_in_dim.54), channel_id=1, replica_groups=mesh['ctx_0'=4,'ctx_1'=4,'ctx_2'=2,'ctx_3'=2,'head'=2] {'ctx_3'}, dimensions={0} | all-to-all | bytes 6291456 | tf_op jit(solution)/shard_map/all_to_all | solution.py:13
  60.5 1.7 copy-done.1
  62.2 1.5 convert_bitcast_fusion.1
  63.7 1.3 copy.112
  66.1 41.9 %while.22 = (s32[]{:T(128)}, bf16[4,512,256]{2,1,0:T(8,128)(2,1)}, bf16[4,2304,2,128]{1,3,2,0:T(8,128)(2,1)}, s32[4,512]{1,0:T(4,128)S(1)}, bf16[4,512,256]{1,2,...) while((s32[]{:T(128)}, bf16[4,512,256]{2,1,0:T(8,128)(2,1)}, ...), condition=%wide.region_3.4_spmd.clone, body=%wide.region_2.3_spmd.clone.sunk | while | flops 1225656576 | bytes 6841953 | solution.py:168
  67.8 6.9 %fusion.96 = bf16[2,128,512]{2,1,0:T(8,128)(2,1)} fusion(bf16[512,2,128]{0,2,1:T(8,128)(2,1)S(1)} %bitcast.149, pred[512,2304]{1,0:T(8,128)(4,1)S(1)} %broadcast_compare_fusion.4, bf16[4,2304,2,128]{3,1,2,0:T(8,128)(2,1)} %get-tuple-element.370, s32[]{:T(128)} %get-tuple-element.357, bf16[4,2304,2,128]{1,3,2,0:T(8,128)(2,1)} %get-tuple-element.367), kind=kOutput, calls=%fused_computation.4.clone.1 | convolution fusion | flops 1224474624 | bytes 4064256 | tf_op jit(solution)/shard_map/while/body/eval_jaxpr/htp,phd->thd/dot_general | solution.py:160
  74.8 1.1 copy.157
  78.3 6.9 %fusion.96 = bf16[2,128,512]{2,1,0:T(8,128)(2,1)} fusion(bf16[512,2,128]{0,2,1:T(8,128)(2,1)S(1)} %bitcast.149, pred[512,2304]{1,0:T(8,128)(4,1)S(1)} %broadcast_compare_fusion.4, bf16[4,2304,2,128]{3,1,2,0:T(8,128)(2,1)} %get-tuple-element.370, s32[]{:T(128)} %get-tuple-element.357, bf16[4,2304,2,128]{1,3,2,0:T(8,128)(2,1)} %get-tuple-element.367), kind=kOutput, calls=%fused_computation.4.clone.1 | convolution fusion | flops 1224474624 | bytes 4064256 | tf_op jit(solution)/shard_map/while/body/eval_jaxpr/htp,phd->thd/dot_general | solution.py:160
  85.2 1.1 copy.157
  88.8 6.9 %fusion.96 = bf16[2,128,512]{2,1,0:T(8,128)(2,1)} fusion(bf16[512,2,128]{0,2,1:T(8,128)(2,1)S(1)} %bitcast.149, pred[512,2304]{1,0:T(8,128)(4,1)S(1)} %broadcast_compare_fusion.4, bf16[4,2304,2,128]{3,1,2,0:T(8,128)(2,1)} %get-tuple-element.370, s32[]{:T(128)} %get-tuple-element.357, bf16[4,2304,2,128]{1,3,2,0:T(8,128)(2,1)} %get-tuple-element.367), kind=kOutput, calls=%fused_computation.4.clone.1 | convolution fusion | flops 1224474624 | bytes 4064256 | tf_op jit(solution)/shard_map/while/body/eval_jaxpr/htp,phd->thd/dot_general | solution.py:160
  95.7 1.1 copy.157
  99.3 6.9 %fusion.96 = bf16[2,128,512]{2,1,0:T(8,128)(2,1)} fusion(bf16[512,2,128]{0,2,1:T(8,128)(2,1)S(1)} %bitcast.149, pred[512,2304]{1,0:T(8,128)(4,1)S(1)} %broadcast_compare_fusion.4, bf16[4,2304,2,128]{3,1,2,0:T(8,128)(2,1)} %get-tuple-element.370, s32[]{:T(128)} %get-tuple-element.357, bf16[4,2304,2,128]{1,3,2,0:T(8,128)(2,1)} %get-tuple-element.367), kind=kOutput, calls=%fused_computation.4.clone.1 | convolution fusion | flops 1224474624 | bytes 4064256 | tf_op jit(solution)/shard_map/while/body/eval_jaxpr/htp,phd->thd/dot_general | solution.py:160
  106.2 1.1 copy.157
  108.0 1.3 copy.115
  109.3 4.6 %all_to_all.56 = bf16[2,32,32,256]{3,2,1,0:T(8,128)(2,1)S(1)} all-to-all(bf16[2,32,32,256]{3,2,1,0:T(8,128)(2,1)S(1)} %copy.115), channel_id=1, replica_groups=mesh['ctx_0'=4,'ctx_1'=4,'ctx_2'=2,'ctx_3'=2,'head'=2] {'ctx_3'}, dimensions={0} | all-to-all | bytes 2097152 | tf_op jit(solution)/shard_map/all_to_all | solution.py:48
  113.9 1.1 reduce_sum.104
  115.1 20.5 %all_to_all.57 = bf16[32,32,256]{2,1,0:T(8,128)(2,1)S(1)} all-to-all(bf16[32,32,256]{2,1,0:T(8,128)(2,1)} %reduce_sum.104), channel_id=1, replica_groups=mesh['ctx_0'=4,'ctx_1'=4,'ctx_2'=2,'ctx_3'=2,'head'=2] {'ctx_0','ctx_1',..., dimensions={0} | all-to-all | bytes 1048576 | tf_op jit(solution)/shard_map/all_to_all | solution.py:56
  136.5 4.1 %all-to-all-start.5 = ((bf16[32,32,256]{2,1,0:T(8,128)(2,1)}), bf16[32,32,256]{2,1,0:T(8,128)(2,1)S(1)}, u32[]{:S(2)}, u32[]{:S(2)}) async-start(bf16[32,32,256]{2,1,0:T(8,128)(2,1)} %broadcast_in_dim.55), calls=%async_computation.5 | async-start | bytes 1048576 | tf_op jit(solution)/shard_map/all_to_all | solution.py:13
  140.6 3.1 convert_multiply_fusion
  143.7 3.3 mul.170
  147.0 6.0 %all-to-all-done.5 = bf16[32,32,256]{2,1,0:T(8,128)(2,1)S(1)} async-done(((bf16[32,32,256]{2,1,0:T(8,128)(2,1)}), bf16[32,32,256]{2,1,0:T(8,128)(2,1)S(1)}, u32[]{:S(2)}, u32[]{:S(2)}) %all-to-all-start.5) | async-done | bytes 524320 | tf_op jit(solution)/shard_map/all_to_all | solution.py:13
  153.1 4.6 %all_to_all.58 = bf16[2,32,32,256]{3,2,1,0:T(8,128)(2,1)S(1)} all-to-all(bf16[2,32,32,256]{3,2,1,0:T(8,128)(2,1)S(1)} %broadcast_in_dim.56), channel_id=1, replica_groups=mesh['ctx_0'=4,'ctx_1'=4,'ctx_2'=2,'ctx_3'=2,'head'=2] {'ctx_3'}, dimensions={0} | all-to-all | bytes 2097152 | tf_op jit(solution)/shard_map/all_to_all | solution.py:13
  157.7 2.6 copy_convert_fusion
  160.3 3.3 reshape.195
  163.6 4.0 %multiply_reduce_fusion.1 = f32[4,512,2]{2,1,0:T(8,128)S(1)} fusion(f32[4,512,2,128]{3,2,1,0:T(2,128)} %reshape.195), kind=kLoop, calls=%fused_computation.47 | loop fusion | flops 1044480 | bytes 2113536 | tf_op jit(solution)/shard_map/reduce_sum | solution.py:93
  167.8 28.9 %multiply_reduce_fusion = f32[4,512,2]{2,1,0:T(8,128)S(1)} fusion(f32[4,512,2,128]{3,2,1,0:T(2,128)S(1)} %copy-done.3, f32[4,512,2,128]{3,2,1,0:T(2,128)S(1)} %copy-done.2, f32[4,512,2]{2,1,0:T(8,128)S(1)} %add_rsqrt_fusion), kind=kLoop, calls=%fused_computation.46 | loop fusion | flops 1568768 | bytes 4227072 | tf_op jit(solution)/shard_map/reduce_sum | solution.py:100
  196.9 3.9 %mul.173 = f32[4,512,2,128]{3,2,1,0:T(2,128)} broadcast(f32[4,512,2]{2,1,0:T(8,128)S(1)} %broadcast_multiply_fusion), dimensions={0,1,2} | broadcast | bytes 2113536 | tf_op jit(solution)/shard_map/mul | solution.py:100
  200.8 3.9 %mul.174 = f32[4,512,256]{2,1,0:T(8,128)} reshape(f32[4,512,2,128]{3,2,1,0:T(2,128)} %mul.173) | data formatting | bytes 4194304 | tf_op jit(solution)/shard_map/mul | solution.py:100
  204.7 3.9 %mul.165 = f32[4,512,2,128]{3,2,1,0:T(2,128)} broadcast(f32[4,512,2]{2,1,0:T(8,128)S(1)} %add_rsqrt_fusion), dimensions={0,1,2} | broadcast | bytes 2113536 | tf_op jit(solution)/shard_map/mul | solution.py:99
  208.6 3.9 %mul.166 = f32[4,512,256]{2,1,0:T(8,128)} reshape(f32[4,512,2,128]{3,2,1,0:T(2,128)} %mul.165) | data formatting | bytes 4194304 | tf_op jit(solution)/shard_map/mul | solution.py:99
  212.5 5.9 %fusion.39 = (bf16[4,512,256]{2,1,0:T(8,128)(2,1)}, f32[4,512,256]{2,1,0:T(8,128)}) fusion(f32[4,512,256]{2,1,0:T(8,128)} %mul.166, f32[4,512,256]{2,1,0:T(8,128)} %mul.174, bf16[12,64,8,256]{3,2,1,0:T(8,128)(2,1)} %bitcast.142, f32[4,512,256]{2,1,0:T(8,128)} %bitcast.147), kind=kLoop, calls=%fused_computation.45 | loop fusion | flops 4194304 | bytes 11534336 | tf_op jit(solution)/shard_map/convert_element_type | solution.py:102
  219.4 86.2 %while.23 = (s32[]{:T(128)}, bf16[4,512,256]{2,1,0:T(8,128)(2,1)}, bf16[4,2304,2,128]{3,1,2,0:T(8,128)(2,1)}, s32[4,512]{1,0:T(4,128)S(1)}, bf16[4,512,256]{2,1,...) while((s32[]{:T(128)}, bf16[4,512,256]{2,1,0:T(8,128)(2,1)}, ...), condition=%wide.region_9.10_spmd.clone, body=%wide.region_8.9_spmd.clone.sunk | while | flops 1839335680 | bytes 28207212 | solution.py:204
  220.5 6.3 %fusion.102 = f32[2,512,2304]{2,1,0:T(8,128)} fusion(bf16[512,2,128]{0,2,1:T(8,128)(2,1)S(1)} %bitcast.143, bf16[4,2304,2,128]{1,3,2,0:T(8,128)(2,1)} %get-tuple-element.396, s32[]{:T(128)} %get-tuple-element.382), kind=kOutput, calls=%fused_computation.21.clone.1 | convolution fusion | flops 603979776 | bytes 10879488 | tf_op jit(solution)/shard_map/while/body/eval_jaxpr/thd,phd->htp/dot_general | solution.py:190
  228.6 10.6 %fusion.103 = bf16[2,128,512]{2,1,0:T(8,128)(2,1)} fusion(f32[2,512,2304]{2,1,0:T(8,128)} %fusion.102, bf16[512,2,128]{0,2,1:T(8,128)(2,1)S(1)} %bitcast.148, pred[512,2304]{1,0:T(8,128)(4,1)S(1)} %broadcast_compare_fusion.5, bf16[4,2304,2,128]{3,1,2,0:T(8,128)(2,1)} %get-tuple-element.393, s32[]{:T(128)} %get-tuple-element.382), kind=kOutput, calls=%fused_computation.20.clone.1 | convolution fusion | flops 1234173952 | bytes 13501440 | tf_op jit(solution)/shard_map/while/body/eval_jaxpr/htp,phd->thd/dot_general | solution.py:199
  239.1 1.1 copy.159
  242.1 6.3 %fusion.102 = f32[2,512,2304]{2,1,0:T(8,128)} fusion(bf16[512,2,128]{0,2,1:T(8,128)(2,1)S(1)} %bitcast.143, bf16[4,2304,2,128]{1,3,2,0:T(8,128)(2,1)} %get-tuple-element.396, s32[]{:T(128)} %get-tuple-element.382), kind=kOutput, calls=%fused_computation.21.clone.1 | convolution fusion | flops 603979776 | bytes 10879488 | tf_op jit(solution)/shard_map/while/body/eval_jaxpr/thd,phd->htp/dot_general | solution.py:190
  250.1 10.6 %fusion.103 = bf16[2,128,512]{2,1,0:T(8,128)(2,1)} fusion(f32[2,512,2304]{2,1,0:T(8,128)} %fusion.102, bf16[512,2,128]{0,2,1:T(8,128)(2,1)S(1)} %bitcast.148, pred[512,2304]{1,0:T(8,128)(4,1)S(1)} %broadcast_compare_fusion.5, bf16[4,2304,2,128]{3,1,2,0:T(8,128)(2,1)} %get-tuple-element.393, s32[]{:T(128)} %get-tuple-element.382), kind=kOutput, calls=%fused_computation.20.clone.1 | convolution fusion | flops 1234173952 | bytes 13501440 | tf_op jit(solution)/shard_map/while/body/eval_jaxpr/htp,phd->thd/dot_general | solution.py:199
  260.7 1.1 copy.159
  263.6 6.3 %fusion.102 = f32[2,512,2304]{2,1,0:T(8,128)} fusion(bf16[512,2,128]{0,2,1:T(8,128)(2,1)S(1)} %bitcast.143, bf16[4,2304,2,128]{1,3,2,0:T(8,128)(2,1)} %get-tuple-element.396, s32[]{:T(128)} %get-tuple-element.382), kind=kOutput, calls=%fused_computation.21.clone.1 | convolution fusion | flops 603979776 | bytes 10879488 | tf_op jit(solution)/shard_map/while/body/eval_jaxpr/thd,phd->htp/dot_general | solution.py:190
  271.7 10.6 %fusion.103 = bf16[2,128,512]{2,1,0:T(8,128)(2,1)} fusion(f32[2,512,2304]{2,1,0:T(8,128)} %fusion.102, bf16[512,2,128]{0,2,1:T(8,128)(2,1)S(1)} %bitcast.148, pred[512,2304]{1,0:T(8,128)(4,1)S(1)} %broadcast_compare_fusion.5, bf16[4,2304,2,128]{3,1,2,0:T(8,128)(2,1)} %get-tuple-element.393, s32[]{:T(128)} %get-tuple-element.382), kind=kOutput, calls=%fused_computation.20.clone.1 | convolution fusion | flops 1234173952 | bytes 13501440 | tf_op jit(solution)/shard_map/while/body/eval_jaxpr/htp,phd->thd/dot_general | solution.py:199
  285.2 6.3 %fusion.102 = f32[2,512,2304]{2,1,0:T(8,128)} fusion(bf16[512,2,128]{0,2,1:T(8,128)(2,1)S(1)} %bitcast.143, bf16[4,2304,2,128]{1,3,2,0:T(8,128)(2,1)} %get-tuple-element.396, s32[]{:T(128)} %get-tuple-element.382), kind=kOutput, calls=%fused_computation.21.clone.1 | convolution fusion | flops 603979776 | bytes 10879488 | tf_op jit(solution)/shard_map/while/body/eval_jaxpr/thd,phd->htp/dot_general | solution.py:190
  293.3 10.6 %fusion.103 = bf16[2,128,512]{2,1,0:T(8,128)(2,1)} fusion(f32[2,512,2304]{2,1,0:T(8,128)} %fusion.102, bf16[512,2,128]{0,2,1:T(8,128)(2,1)S(1)} %bitcast.148, pred[512,2304]{1,0:T(8,128)(4,1)S(1)} %broadcast_compare_fusion.5, bf16[4,2304,2,128]{3,1,2,0:T(8,128)(2,1)} %get-tuple-element.393, s32[]{:T(128)} %get-tuple-element.382), kind=kOutput, calls=%fused_computation.20.clone.1 | convolution fusion | flops 1234173952 | bytes 13501440 | tf_op jit(solution)/shard_map/while/body/eval_jaxpr/htp,phd->thd/dot_general | solution.py:199
  305.6 1.3 copy.123
  307.0 4.7 %all_to_all.59 = bf16[2,32,4,8,256]{4,3,2,1,0:T(8,128)(2,1)S(1)} all-to-all(bf16[2,32,4,8,256]{4,3,2,1,0:T(8,128)(2,1)S(1)} %copy.123), channel_id=1, replica_groups=mesh['ctx_0'=4,'ctx_1'=4,'ctx_2'=2,'ctx_3'=2,'head'=2] {'ctx_3'}, dimensions={0} | all-to-all | bytes 2097152 | tf_op jit(solution)/shard_map/all_to_all | solution.py:48
  311.7 1.1 reduce_sum.108
  312.9 3.9 %all-to-all-start.8 = ((bf16[32,4,8,256]{3,2,1,0:T(8,128)(2,1)}), bf16[32,4,8,256]{3,2,1,0:T(8,128)(2,1)S(1)}, u32[]{:S(2)}, u32[]{:S(2)}) async-start(bf16[32,4,8,256]{3,2,1,0:T(8,128)(2,1)} %reduce_sum.108), calls=%async_computation.8 | async-start | bytes 1048576 | tf_op jit(solution)/shard_map/all_to_all | solution.py:56
  316.8 14.1 %all-to-all-done.8 = bf16[32,4,8,256]{3,2,1,0:T(8,128)(2,1)S(1)} async-done(((bf16[32,4,8,256]{3,2,1,0:T(8,128)(2,1)}), bf16[32,4,8,256]{3,2,1,0:T(8,128)(2,1)S(1)}, u32[]{:S(2)}, u32[]{:S(2)}) %all-to-all-start.8) | async-done | bytes 524320 | tf_op jit(solution)/shard_map/all_to_all | solution.py:56
  331.2 1.2 fusion.40
  332.4 6.5 %all_to_all.60 = bf16[2,32,512]{2,1,0:T(8,128)(2,1)S(1)} all-to-all(bf16[2,32,512]{2,1,0:T(8,128)(2,1)S(1)} %broadcast_in_dim.57), channel_id=1, replica_groups=mesh['ctx_0'=4,'ctx_1'=4,'ctx_2'=2,'ctx_3'=2,'head'=2] {'head'}, dimensions={0} | all-to-all | bytes 131072 | tf_op jit(solution)/shard_map/all_to_all | solution.py:13
  339.9 1.4 mul.187
  341.3 1.9 multiply_convert_fusion
  343.4 6.3 %fusion.33 = bf16[4,8,4,2048]{3,1,2,0:T(8,128)(2,1)S(1)} fusion(bf16[2048,2048]{1,0:T(8,128)(2,1)} %param.15, bf16[4,8,4,2048]{3,2,1,0:T(4,128)(2,1)S(1)} %dot_general.52), kind=kOutput, calls=%fused_computation.41 | convolution fusion | flops 1074003968 | bytes 9437184 | tf_op jit(solution)/shard_map/dot_general | solution.py:85
  349.7 9.0 %all_to_all.61 = bf16[2,4,8,2,2048]{4,2,3,1,0:T(8,128)(2,1)S(1)} all-to-all(bf16[2,4,8,2,2048]{4,2,3,1,0:T(8,128)(2,1)S(1)} %bitcast.155), channel_id=1, replica_groups=mesh['ctx_0'=4,'ctx_1'=4,'ctx_2'=2,'ctx_3'=2,'head'=2] {'head'}, dimensions={0} | all-to-all | bytes 1048576 | tf_op jit(solution)/shard_map/all_to_all | solution.py:48
  (108 shorter events, 35.6 us)
Async XLA Ops:
  0.0 7.0 %copy-start = (bf16[2048,512]{1,0:T(8,128)(2,1)S(1)}, bf16[2048,512]{1,0:T(8,128)(2,1)}, u32[]{:S(2)}) copy-start(bf16[2048,512]{1,0:T(8,128)(2,1)} %param.16) | copy-start | bytes 6291460
  6.0 1.0 copy-start.4
  7.0 4.8 %copy-start.12 = (bf16[256,512]{1,0:T(8,128)(2,1)S(1)}, bf16[256,512]{1,0:T(8,128)(2,1)}, u32[]{:S(2)}) copy-start(bf16[256,512]{1,0:T(8,128)(2,1)} %param.19) | copy-start | bytes 786436
  7.0 4.8 %copy-start.14 = (bf16[4,8,512]{2,1,0:T(8,128)(2,1)S(1)}, bf16[4,8,512]{2,1,0:T(8,128)(2,1)}, u32[]{:S(2)}) copy-start(bf16[4,8,512]{2,1,0:T(8,128)(2,1)} %param.23) | copy-start | bytes 98308
  7.0 9.3 %copy-start.7 = (bf16[512,256]{1,0:T(8,128)(2,1)S(1)}, bf16[512,256]{1,0:T(8,128)(2,1)}, u32[]{:S(2)}) copy-start(bf16[512,256]{1,0:T(8,128)(2,1)} %param.18) | copy-start | bytes 786436
  7.0 9.5 %copy-start.5 = (bf16[512,256]{1,0:T(8,128)(2,1)S(1)}, bf16[512,256]{1,0:T(8,128)(2,1)}, u32[]{:S(2)}) copy-start(bf16[512,256]{1,0:T(8,128)(2,1)} %param.17) | copy-start | bytes 786436
  8.4 7.8 %all-to-all-start = ((f32[2,32,512]{2,1,0:T(8,128)}), f32[2,32,512]{2,1,0:T(8,128)S(1)}, u32[]{:S(2)}, u32[]{:S(2)}) async-start(f32[2,32,512]{2,1,0:T(8,128)} %broadcast_in_dim.52), calls=%async_computation | async-start | bytes 262144 | tf_op jit(solution)/shard_map/all_to_all | solution.py:13
  16.4 19.2 %copy-start.8 = (f32[32,256]{1,0:T(8,128)}, f32[32,256]{1,0:T(8,128)S(1)}, u32[]{:S(2)}) copy-start(f32[32,256]{1,0:T(8,128)S(1)} %fusion.60) | copy-start | bytes 98308
  16.6 19.1 %copy-start.10 = (f32[32,256]{1,0:T(8,128)}, f32[32,256]{1,0:T(8,128)S(1)}, u32[]{:S(2)}) copy-start(f32[32,256]{1,0:T(8,128)S(1)} %fusion.61) | copy-start | bytes 98308
  18.0 34.1 %all-to-all-start.1 = ((bf16[32,12,8,256]{3,2,1,0:T(8,128)(2,1)}), bf16[32,12,8,256]{3,2,1,0:T(8,128)(2,1)}, u32[]{:S(2)}, u32[]{:S(2)}) async-start(bf16[32,12,8,256]{3,2,1,0:T(8,128)(2,1)} %broadcast_in_dim.53), calls=%async_computation.1 | async-start | bytes 3145728 | tf_op jit(solution)/shard_map/all_to_all | solution.py:13
  60.5 1.7 copy-start.1
  62.2 3.9 %copy-start.13 = (s32[4,512]{1,0:T(4,128)S(1)}, s32[4,512]{1,0:T(4,128)}, u32[]{:S(2)}) copy-start(s32[4,512]{1,0:T(4,128)} %param.22) | copy-start | bytes 24580
  136.5 16.5 %all-to-all-start.5 = ((bf16[32,32,256]{2,1,0:T(8,128)(2,1)}), bf16[32,32,256]{2,1,0:T(8,128)(2,1)S(1)}, u32[]{:S(2)}, u32[]{:S(2)}) async-start(bf16[32,32,256]{2,1,0:T(8,128)(2,1)} %broadcast_in_dim.55), calls=%async_computation.5 | async-start | bytes 1048576 | tf_op jit(solution)/shard_map/all_to_all | solution.py:13
  163.6 4.2 %copy-start.2 = (f32[4,512,2,128]{3,2,1,0:T(2,128)S(1)}, f32[4,512,2,128]{3,2,1,0:T(2,128)}, u32[]{:S(2)}) copy-start(f32[4,512,2,128]{3,2,1,0:T(2,128)} %reshape.195) | copy-start | bytes 6291460
  163.6 4.2 %copy-start.3 = (f32[4,512,2,128]{3,2,1,0:T(2,128)S(1)}, f32[4,512,2,128]{3,2,1,0:T(2,128)}, u32[]{:S(2)}) copy-start(f32[4,512,2,128]{3,2,1,0:T(2,128)} %mul.170) | copy-start | bytes 6291460
  307.0 24.0 %copy-start.6 = (bf16[512,256]{1,0:T(8,128)(2,1)S(1)}, bf16[512,256]{1,0:T(8,128)(2,1)}, u32[]{:S(2)}) copy-start(bf16[512,256]{1,0:T(8,128)(2,1)} %param.17) | copy-start | bytes 786436
  307.0 24.0 %copy-start.11 = (f32[32,256]{1,0:T(8,128)S(1)}, f32[32,256]{1,0:T(8,128)}, u32[]{:S(2)}) copy-start(f32[32,256]{1,0:T(8,128)} %copy-done.10) | copy-start | bytes 98308
  307.0 24.2 %copy-start.9 = (f32[32,256]{1,0:T(8,128)S(1)}, f32[32,256]{1,0:T(8,128)}, u32[]{:S(2)}) copy-start(f32[32,256]{1,0:T(8,128)} %copy-done.8) | copy-start | bytes 98308
  312.9 18.0 %all-to-all-start.8 = ((bf16[32,4,8,256]{3,2,1,0:T(8,128)(2,1)}), bf16[32,4,8,256]{3,2,1,0:T(8,128)(2,1)S(1)}, u32[]{:S(2)}, u32[]{:S(2)}) async-start(bf16[32,4,8,256]{3,2,1,0:T(8,128)(2,1)} %reduce_sum.108), calls=%async_computation.8 | async-start | bytes 1048576 | tf_op jit(solution)/shard_map/all_to_all | solution.py:56
where the time goes:
time: 362 us; the launch traced here: 360 us
  matrix products  109 us (30%)
  local copies, waits for them, and re-layouts  87.2 us (24%)
  other arithmetic  56.9 us (16%)
  blocking collectives  56.1 us (15%)
  waiting for transfers between devices  27.5 us (8%)
  starting transfers between devices  22.2 us (6%)
    dot_general x4, matrix products, backward_user(): jnp.einsum('htp,phd->thd', grad_scores, user_keys, preferred_element_type...  42.3 us
    reduce_sum x1, other arithmetic, norm_grads(): jnp.mean(normed_grad * normed, axis=-1, keepdims=True)  28.9 us
    dot_general x4, matrix products, forward_user(): jnp.einsum('htp,phd->thd', weights, user_values, preferred_element_type=j...  27.8 us
    dot_general x4, matrix products, backward_user(): jnp.einsum('thd,phd->htp', user_grads.reshape(row_count, heads_here, DH),...  25.3 us
    unnamed x34, local copies, waits for them, and re-layouts  24.2 us
    all_to_all x1, blocking collectives, summed_rows_2(): lax.all_to_all(nearer.astype(jnp.bfloat16), far, split_axis=0, concat_axi...  20.5 us
    all_to_all x3, starting transfers between devices, from_everyone(): return lax.all_to_all(copies, axis, split_axis=0, concat_axis=0, tiled=True)  18.3 us
    all_to_all x3, blocking collectives, sent_and_summed(): blocks = lax.all_to_all(cut_along(shard, dim, size), axis, 0, 0, tiled=True)  18.3 us
  transfers between devices with their start and end apart: 4, of which 4 were waited for; matrix products, arithmetic and copies ran while one was open for 7% of the time, Pallas kernels for 0%

commit v1 on v0

v1 whole, which is shorter than its diff:
```python
import jax
import jax.numpy as jnp
from jax import lax
from jax.experimental import pallas as pl
from jax.experimental.pallas import tpu as pltpu
from jax.sharding import Mesh
from jax.sharding import PartitionSpec as P

DH = 128
CTX = ("x", "y", "zh", "c")
BF = jnp.bfloat16
F32 = jnp.float32
LAST = (((1,), (1,)), ((), ()))
USERS, ROWS, EACH, WIDTH = 4, 8, 4, 2048
HALF, MODEL, LOCAL = 2048, 512, 256
TARGETS, EVENTS = 512, 2304
OWN = USERS * ROWS
CUT_ROWS = 128
HID_CHUNKS = 4
HID_CHUNK = HALF // HID_CHUNKS
OUT_CHUNKS = 4
OUT_CHUNK = WIDTH // OUT_CHUNKS
SCALE = DH**-0.5


def contract_last(left, right):
    return lax.dot_general(left, right, LAST, preferred_element_type=F32)


def dot(left, right):
    return jnp.dot(left, right, preferred_element_type=F32)


def silu(v):
    return v * jax.nn.sigmoid(v)


def silu_slope(v):
    s = jax.nn.sigmoid(v)
    return s * (1.0 + v * (1.0 - s))


def kernel(
    x_hbm, wh_hbm, we_hbm, wq_hbm, wg_hbm, wp_hbm, k_hbm, v_hbm, cut_hbm, cot_hbm,
    out_ref,
    x_v, wh_v, we_v, wq_v, wg_v, wp_v, k_v, v_v, cut_v, cot_v,
    slope_v, hid_slope, enc_send, enc_recv, lin_q, lin_g, gates_v, outg_v, gateg_v, qgrad_v,
    ag1, ag2, rs1_send, rs1_recv, rs2_send, rs2_recv,
    emb_send, emb_recv, part_send, part_recv, part_own,
    load_sem, kv_sem, ag_ssem, ag_rsem, rs_ssem, rs_rsem, head_ssem, head_rsem,
):
    xi, yi, zi, ci, hi = (lax.axis_index(a) for a in (*CTX, "head"))
    i1 = yi * 2 + ci
    i2 = xi * 2 + zi
    base = (((xi * 4 + yi) * 2 + zi) * 2 + ci) * EVENTS
    partner = {"head": 1 - hi}

    def id1(p):
        return {"y": p // 2, "c": lax.rem(p, 2)}

    def id2(p):
        return {"x": p // 2, "zh": lax.rem(p, 2)}

    barrier = pltpu.get_barrier_semaphore()
    pl.semaphore_signal(barrier, inc=1, device_id=partner, device_id_type=pl.DeviceIdType.MESH)
    for k in range(1, 8):
        for me, ids in ((i1, id1), (i2, id2)):
            pl.semaphore_signal(
                barrier, inc=1, device_id=ids(lax.rem(me + k, 8)),
                device_id_type=pl.DeviceIdType.MESH,
            )

    loads = [pltpu.make_async_copy(x_hbm, x_v, load_sem.at[0])]
    for j in range(HID_CHUNKS):
        cols = pl.ds(j * HID_CHUNK, HID_CHUNK)
        loads.append(
            pltpu.make_async_copy(wh_hbm.at[:, cols], wh_v.at[:, cols], load_sem.at[len(loads)])
        )
    for src, dst in (
        (we_hbm, we_v), (cot_hbm, cot_v), (wp_hbm, wp_v), (wq_hbm, wq_v), (wg_hbm, wg_v),
        (cut_hbm, cut_v),
    ):
        loads.append(pltpu.make_async_copy(src, dst, load_sem.at[len(loads)]))
    for copy in loads:
        copy.start()

    def kv_copies(u):
        return (
            pltpu.make_async_copy(k_hbm.at[u], k_v.at[u], kv_sem.at[0, u]),
            pltpu.make_async_copy(v_hbm.at[u], v_v.at[u], kv_sem.at[1, u]),
        )

    for u in range(USERS):
        for copy in kv_copies(u):
            copy.start()

    loads[0].wait()
    for j in range(HID_CHUNKS):
        loads[1 + j].wait()
        cols = slice(j * HID_CHUNK, (j + 1) * HID_CHUNK)
        lin = dot(x_v[...], wh_v[:, cols])
        s = jax.nn.sigmoid(lin)
        hidden = lin * s
        hid_slope[:, cols] = s * (1.0 + lin * (1.0 - s))
        if j == 0:
            loads[1 + HID_CHUNKS].wait()
        part = dot(hidden.astype(BF), we_v[cols, :])
        total = part if j == 0 else total + part
    enc_send[...] = total[0:32] + total[32:64] + total[64:96] + total[96:128]

    pl.semaphore_wait(barrier, 15)

    def head_copy(src, dst, n):
        return pltpu.make_async_remote_copy(
            src_ref=src, dst_ref=dst, send_sem=head_ssem.at[n], recv_sem=head_rsem.at[n],
            device_id=partner, device_id_type=pl.DeviceIdType.MESH,
        )

    enc_copy = head_copy(enc_send, enc_recv, 0)
    enc_copy.start()
    for n in range(2 + HID_CHUNKS, 7 + HID_CHUNKS):
        loads[n].wait()
    cot = cot_v[...].astype(F32).reshape(OWN, MODEL).astype(BF)
    outg_v[...] = contract_last(cot, wp_v[...]).astype(BF).astype(F32)
    enc_copy.wait()
    embedded = (0.5 * (enc_send[...] + enc_recv[...])).astype(BF)
    query_lin = dot(embedded, wq_v[...])
    lin_q[...] = silu_slope(query_lin)
    queries = silu(query_lin).astype(BF).astype(F32)

    def send_seven(src, dst, ssem, rsem, me, ids):
        for k in range(1, 8):
            peer = lax.rem(me + k, 8)
            pltpu.make_async_remote_copy(
                src_ref=src(peer), dst_ref=dst, send_sem=ssem, recv_sem=rsem,
                device_id=ids(peer), device_id_type=pl.DeviceIdType.MESH,
            ).start()

    def seven(ref, ssem, rsem):
        return pltpu.make_async_remote_copy(
            src_ref=ref, dst_ref=ref, send_sem=ssem, recv_sem=rsem,
            device_id=partner, device_id_type=pl.DeviceIdType.MESH,
        )

    def gather_first(ph, u, block):
        rows = pl.ds(pl.multiple_of(i2 * ROWS, ROWS), ROWS)
        ag1[ph, u, rows, :] = block
        ref = ag1.at[ph, u, rows, :]
        send_seven(lambda p: ref, ref, ag_ssem.at[ph, u, 0], ag_rsem.at[ph, u, 0], i2, id2)

    def gather_second(ph, u):
        seven(ag1.at[ph, u, 0:56, :], ag_ssem.at[ph, u, 0], ag_rsem.at[ph, u, 0]).wait_recv()
        rows = pl.ds(pl.multiple_of(i1 * 64, 64), 64)
        ag2[ph, u, rows, :] = ag1[ph, u].astype(BF)
        ref = ag2.at[ph, u, rows, :]
        send_seven(lambda p: ref, ref, ag_ssem.at[ph, u, 1], ag_rsem.at[ph, u, 1], i1, id1)

    def gather_end(ph, u):
        seven(ag2.at[ph, u, 0:448, :], ag_ssem.at[ph, u, 1], ag_rsem.at[ph, u, 1]).wait_recv()

    def sum_first(ph, u):
        mine = pl.ds(pl.multiple_of(i1 * 64, 64), 64)
        rs1_recv[ph, u, mine, :] = rs1_send[ph, u, mine, :]
        send_seven(
            lambda p: rs1_send.at[ph, u, pl.ds(pl.multiple_of(p * 64, 64), 64), :],
            rs1_recv.at[ph, u, mine, :],
            rs_ssem.at[ph, u, 0], rs_rsem.at[ph, u, 0], i1, id1,
        )

    def sum_second(ph, u):
        seven(rs1_recv.at[ph, u, 0:448, :], rs_ssem.at[ph, u, 0], rs_rsem.at[ph, u, 0]).wait_recv()
        total = rs1_recv[ph, u, 0:64, :].astype(F32)
        for g in range(1, 8):
            total = total + rs1_recv[ph, u, g * 64 : (g + 1) * 64, :].astype(F32)
        rs2_send[ph, u] = total
        mine = pl.ds(pl.multiple_of(i2 * ROWS, ROWS), ROWS)
        rs2_recv[ph, u, mine, :] = rs2_send[ph, u, mine, :]
        send_seven(
            lambda p: rs2_send.at[ph, u, pl.ds(pl.multiple_of(p * ROWS, ROWS), ROWS), :],
            rs2_recv.at[ph, u, mine, :],
            rs_ssem.at[ph, u, 1], rs_rsem.at[ph, u, 1], i2, id2,
        )

    def sum_end(ph, u):
        seven(rs2_recv.at[ph, u, 0:56, :], rs_ssem.at[ph, u, 1], rs_rsem.at[ph, u, 1]).wait_recv()
        total = rs2_recv[ph, u, 0:8, :]
        for g in range(1, 8):
            total = total + rs2_recv[ph, u, g * 8 : (g + 1) * 8, :]
        return total

    for u in range(USERS):
        gather_first(0, u, queries[u * ROWS : (u + 1) * ROWS])
    gate_lin = dot(embedded, wg_v[...])
    lin_g[...] = silu_slope(gate_lin)
    gates_v[...] = silu(gate_lin).astype(BF).astype(F32)
    for u in range(USERS):
        gather_second(0, u)

    def own_rows(u):
        return pl.ds(pl.multiple_of(u * ROWS, ROWS), ROWS)

    def norm_and_gather(u):
        attended = sum_end(0, u)
        rows = own_rows(u)
        grads = outg_v[rows, :]
        gates = gates_v[rows, :]
        blocks, gate_blocks = [], []
        for h in range(2):
            cols = slice(h * DH, (h + 1) * DH)
            a, g, gate = attended[:, cols], grads[:, cols], gates[:, cols]
            rscale = lax.rsqrt(jnp.mean(a * a, axis=-1, keepdims=True) + 1e-06)
            normed = a * rscale
            gate_blocks.append(g * normed)
            ng = g * gate
            grad = rscale * (ng - normed * jnp.mean(ng * normed, axis=-1, keepdims=True))
            blocks.append(grad.astype(BF).astype(F32))
        gateg_v[rows, :] = jnp.concatenate(gate_blocks, axis=1)
        gather_first(1, u, jnp.concatenate(blocks, axis=1))

    def query_grad_end(u):
        qgrad_v[own_rows(u), :] = sum_end(1, u) * SCALE

    lane = lax.broadcasted_iota(jnp.int32, (1, EVENTS), 1) + base

    def forward(u, h):
        cols = pl.ds(pl.multiple_of(h * DH, DH), DH)
        for r in range(0, TARGETS, CUT_ROWS):
            rows = slice(r, r + CUT_ROWS)
            scores = contract_last(ag2[0, u, rows, cols], k_v[u, :, cols])
            cut = cut_v[u, rows, :]
            visible = lane < jnp.concatenate([cut] * (EVENTS // DH), axis=1)
            y = jnp.where(visible, scores * (0.5 * SCALE), -1e30).astype(BF)
            t = jnp.tanh(y)
            s2 = BF(1) + t
            w = y * s2
            slope_v[u * 2 + h, rows, :] = BF(0.5) * s2 + w * (BF(0.5) - BF(0.5) * t)
            rs1_send[0, u, rows, cols] = dot(w, v_v[u, :, cols]).astype(BF)

    def backward(u, h):
        cols = pl.ds(pl.multiple_of(h * DH, DH), DH)
        for r in range(0, TARGETS, CUT_ROWS):
            rows = slice(r, r + CUT_ROWS)
            wgrad = contract_last(ag2[1, u, rows, cols], v_v[u, :, cols])
            gs = wgrad.astype(BF) * slope_v[u * 2 + h, rows, :]
            rs1_send[1, u, rows, cols] = dot(gs, k_v[u, :, cols]).astype(BF)

    @pl.loop(0, 2 * USERS)
    def _(i):
        u = i // 2
        h = lax.rem(i, 2)

        @pl.when(h == 0)
        def _():
            gather_end(0, u)
            for copy in kv_copies(u):
                copy.wait()

        forward(u, h)

        @pl.when(h == 1)
        def _():
            sum_first(0, u)

            @pl.when(u >= 1)
            def _():
                norm_and_gather(u - 1)

        @pl.when((h == 0) & (u >= 1))
        def _():
            sum_second(0, u - 1)

            @pl.when(u >= 2)
            def _():
                gather_second(1, u - 2)

    @pl.loop(0, 2 * USERS)
    def _(i):
        u = i // 2
        h = lax.rem(i, 2)

        @pl.when(h == 0)
        def _():
            gather_end(1, u)

        backward(u, h)

        @pl.when(h == 1)
        def _():
            sum_first(1, u)

        @pl.when(i == 0)
        def _():
            sum_second(0, USERS - 1)
            gather_second(1, USERS - 2)

        @pl.when(i == 1)
        def _():
            norm_and_gather(USERS - 1)

        @pl.when(i == 2)
        def _():
            gather_second(1, USERS - 1)

        @pl.when((h == 0) & (u >= 1))
        def _():
            sum_second(1, u - 1)

        @pl.when((h == 1) & (u >= 1))
        def _():
            query_grad_end(u - 1)

    sum_second(1, USERS - 1)
    query_grad_end(USERS - 1)

    query_back = (qgrad_v[...] * lin_q[...]).astype(BF)
    gate_back = (gateg_v[...] * lin_g[...]).astype(BF)
    emb_send[...] = (
        contract_last(query_back, wq_v[...]) + contract_last(gate_back, wg_v[...])
    ).astype(BF)
    emb_copy = head_copy(emb_send, emb_recv, 1)
    emb_copy.start()
    emb_copy.wait()
    embed_grad = (0.5 * (emb_send[...].astype(F32) + emb_recv[...].astype(F32))).astype(BF)
    hidden_grad = contract_last(embed_grad, we_v[...])
    hidden_back = jnp.concatenate(
        [(hidden_grad * hid_slope[r * OWN : (r + 1) * OWN, :]).astype(BF) for r in range(EACH)],
        axis=0,
    )
    x_v[...] = hidden_back
    mine = pl.ds(pl.multiple_of(hi * 64, 64), 64)
    other = pl.ds(pl.multiple_of((1 - hi) * 64, 64), 64)
    copies = []
    for j in range(OUT_CHUNKS):
        cols = slice(j * OUT_CHUNK, (j + 1) * OUT_CHUNK)
        part_own[:, cols] = contract_last(x_v[...], wh_v[cols, :])
        part_send[j] = part_own[other, cols].astype(BF)
        copies.append(head_copy(part_send.at[j], part_recv.at[j], 2 + j))
        copies[-1].start()
    for j in range(OUT_CHUNKS):
        cols = slice(j * OUT_CHUNK, (j + 1) * OUT_CHUNK)
        copies[j].wait()
        own = part_own[mine, cols].astype(BF).astype(F32)
        out_ref[:, cols] = (own + part_recv[j].astype(F32)).astype(BF)

    @pl.loop(0, USERS)
    def _(u):
        for ph in range(2):
            seven(ag1.at[ph, u, 0:56, :], ag_ssem.at[ph, u, 0], ag_rsem.at[ph, u, 0]).wait_send()
            seven(ag2.at[ph, u, 0:448, :], ag_ssem.at[ph, u, 1], ag_rsem.at[ph, u, 1]).wait_send()
            seven(rs1_send.at[ph, u, 0:448, :], rs_ssem.at[ph, u, 0], rs_rsem.at[ph, u, 0]).wait_send()
            seven(rs2_send.at[ph, u, 0:56, :], rs_ssem.at[ph, u, 1], rs_rsem.at[ph, u, 1]).wait_send()


def body(
    content_rows, w_hidden, w_embed, w_query, w_gate, w_proj,
    history_keys, history_values, cutoffs, out_cotangent,
):
    x = content_rows.transpose(2, 0, 1, 3).reshape(EACH * OWN, WIDTH)
    cut = cutoffs.reshape(USERS, 4, 4, 2, 2, ROWS).transpose(0, 2, 4, 1, 3, 5)
    cut = jnp.broadcast_to(cut.reshape(USERS, TARGETS, 1), (USERS, TARGETS, DH))
    dma = pltpu.SemaphoreType.DMA
    v = pltpu.VMEM
    part = pl.pallas_call(
        kernel,
        name="attention_and_encoder",
        out_shape=jax.ShapeDtypeStruct((64, WIDTH), BF),
        in_specs=[pl.BlockSpec(memory_space=pl.ANY)] * 10,
        out_specs=pl.BlockSpec(memory_space=pltpu.VMEM),
        scratch_shapes=[
            v((EACH * OWN, WIDTH), BF), v((WIDTH, HALF), BF), v((HALF, MODEL), BF),
            v((MODEL, LOCAL), BF), v((MODEL, LOCAL), BF), v((LOCAL, MODEL), BF),
            v((USERS, EVENTS, LOCAL), BF), v((USERS, EVENTS, LOCAL), BF),
            v((USERS, TARGETS, DH), jnp.int32), v((USERS, ROWS, MODEL), BF),
            v((2 * USERS, TARGETS, EVENTS), BF), v((EACH * OWN, HALF), F32),
            v((OWN, MODEL), F32), v((OWN, MODEL), F32),
            v((OWN, LOCAL), F32), v((OWN, LOCAL), F32), v((OWN, LOCAL), F32),
            v((OWN, LOCAL), F32), v((OWN, LOCAL), F32), v((OWN, LOCAL), F32),
            v((2, USERS, 64, LOCAL), F32), v((2, USERS, TARGETS, LOCAL), BF),
            v((2, USERS, TARGETS, LOCAL), BF), v((2, USERS, TARGETS, LOCAL), BF),
            v((2, USERS, 64, LOCAL), F32), v((2, USERS, 64, LOCAL), F32),
            v((OWN, MODEL), BF), v((OWN, MODEL), BF),
            v((OUT_CHUNKS, 64, OUT_CHUNK), BF), v((OUT_CHUNKS, 64, OUT_CHUNK), BF),
            v((EACH * OWN, WIDTH), F32),
            dma((7 + HID_CHUNKS,)), dma((2, USERS)),
            dma((2, USERS, 2)), dma((2, USERS, 2)), dma((2, USERS, 2)), dma((2, USERS, 2)),
            dma((2 + OUT_CHUNKS,)), dma((2 + OUT_CHUNKS,)),
        ],
        compiler_params=pltpu.CompilerParams(
            collective_id=0, has_side_effects=True, vmem_limit_bytes=62 * 2**20
        ),
    )(
        x, w_hidden, w_embed, w_query, w_gate, w_proj,
        history_keys, history_values, cut, out_cotangent,
    )
    return part.reshape(2, USERS, ROWS, WIDTH).transpose(1, 2, 0, 3)


def solution(mesh):
    split = Mesh(
        mesh.devices.reshape(4, 4, 2, 2, mesh.shape["head"]),
        (*CTX, "head"),
    )
    return jax.shard_map(
        body,
        mesh=split,
        in_specs=(
            P(None, CTX, None, None), P(None, "head"), P("head", None), P(None, "head"),
            P(None, "head"), P("head", None), P(None, CTX, "head"), P(None, CTX, "head"),
            P(), P(None, CTX, None),
        ),
        out_specs=P(None, CTX, "head", None),
        check_vma=False,
    )
```

time: 362 us -> 114 us (0.31)
  matrix products: 109 us -> 0 us
  Pallas kernels: 0 us -> 108 us
  local copies, waits for them, and re-layouts: 87.2 us -> 6.61 us
  other arithmetic: 56.9 us -> 0 us
  blocking collectives: 56.1 us -> 0 us
  waiting for transfers between devices: 27.5 us -> 0 us
  starting transfers between devices: 22.2 us -> 0 us
    dot_general x21 -> x0, matrix products: 109 us -> none  [the longest x4 42.3 us: backward_user(): jnp.einsum('htp,phd->thd', grad_scores, user_keys, preferred_element_type...]
    pallas_call x0 -> x1, Pallas kernels: none -> 108 us  [body(): pl.pallas_call(kernel, name='attention_and_encoder', out_shape=jax.ShapeD...]
    all_to_all x7 -> x0, blocking collectives: 56.1 us -> none  [the longest x1 20.5 us: summed_rows_2(): lax.all_to_all(nearer.astype(jnp.bfloat16), far, split_axis=0, concat_axi...]
    reduce_sum x10 -> x0, other arithmetic: 35.7 us -> none  [the longest x1 28.9 us: norm_grads(): jnp.mean(normed_grad * normed, axis=-1, keepdims=True)]
    all_to_all x4 -> x0, waiting for transfers between devices: 27.5 us -> none  [the longest x1 14.1 us: summed_rows_2(): lax.all_to_all(nearer.astype(jnp.bfloat16), far, split_axis=0, concat_axi...]
    unnamed x34 -> x0, local copies, waits for them, and re-layouts: 24.2 us -> none
    all_to_all x4 -> x0, starting transfers between devices: 22.2 us -> none  [the longest x3 18.3 us: from_everyone(): return lax.all_to_all(copies, axis, split_axis=0, concat_axis=0, tiled=True)]
    mul x7 -> x0, local copies, waits for them, and re-layouts: 20.6 us -> none  [the longest x2 7.82 us: norm_grads(): normed * jnp.mean(normed_grad * normed, axis=-1, keepdims=True)]
  transfers between devices with their start and end apart: 4 -> 0, of which waited for: 4 -> 0; matrix products, arithmetic and copies ran while one was open for 7% -> 0% of each run, Pallas kernels for 0% -> 0%
where the time goes in v1:
time: 114 us
  Pallas kernels  108 us (95%)
  local copies, waits for them, and re-layouts  6.61 us (6%)
    pallas_call x1, Pallas kernels, body(): pl.pallas_call(kernel, name='attention_and_encoder', out_shape=jax.ShapeD...  108 us

profile of v1, /device:TPU:0, one launch (start us, length us, event | category | flops | bytes accessed | tf_op | source)
XLA Modules:
  0.0 114.2 jit_solution(1493411131946820714)
XLA Ops:
  0.0 0.9 reshape.12
  0.9 0.1 copy.12
  1.0 0.2 broadcast_in_dim.7
  1.2 2.2 %copy.11 = bf16[4,4,8,2048]{3,2,1,0:T(8,128)(2,1)} copy(bf16[4,4,8,2048]{3,0,2,1:T(4,128)(2,1)} %bitcast.9) | data formatting | bytes 1048576 | tf_op jit(solution)/shard_map/transpose | solution.py:358
  3.4 1.3 %broadcast_in_dim.8.cut_hbm = s32[4,512,128]{2,1,0:T(8,128)} broadcast(s32[4,512]{1,0:T(4,128)S(1)} %broadcast_in_dim.7), dimensions={0,1} | broadcast | bytes 1056768 | tf_op jit(solution)/shard_map/broadcast_in_dim | solution.py:360
  4.7 107.6 %attention_and_encoder.1 = bf16[64,2048]{1,0:T(8,128)(2,1)} custom-call(bf16[128,2048]{1,0:T(8,128)(2,1)} %bitcast.7, bf16[2048,2048]{1,0:T(8,128)(2,1)} %wh_hbm.1, bf16[2048,512]{1,0:T(8,128)(2,1)} %we_hbm.1, bf16[512,256]{1,0:T(8,128)(2,1)} %wq_hbm.1, bf16[512,256]{1,0:T(8,128)(2,1)} %wg_hbm.1, bf16[256,512]{1,0:T(8,128)(2,1)} %wp_hbm.1, ...), custom_call_target="tpu_custom_call" | custom-call | tf_op jit(solution)/shard_map/attention_and_encoder/pallas_call | solution.py:363
  112.3 1.9 %copy.15 = bf16[2,4,8,2048]{3,0,2,1:T(2,128)(2,1)} copy(bf16[2,4,8,2048]{3,2,1,0:T(8,128)(2,1)} %bitcast.8) | data formatting | bytes 524288 | tf_op jit(solution)/shard_map/reshape | solution.py:395

commit v2 on v1

v2 whole, which is shorter than its diff:
```python
import jax
import jax.numpy as jnp
from jax import lax
from jax.experimental import pallas as pl
from jax.experimental.pallas import tpu as pltpu
from jax.sharding import Mesh
from jax.sharding import PartitionSpec as P

DH = 128
CTX = ("x", "y", "zh", "c")
BF = jnp.bfloat16
F32 = jnp.float32
LAST = (((1,), (1,)), ((), ()))
USERS, ROWS, EACH, WIDTH = 4, 8, 4, 2048
HALF, MODEL, LOCAL = 2048, 512, 256
TARGETS, EVENTS = 512, 2304
OWN = USERS * ROWS
SLOTS, NEAR = 64, 32
OFFSETS = sorted(
    [(a, b, c) for a in range(4) for b in range(4) for c in range(2) if a or b or c],
    key=lambda t: -(min(t[0], 4 - t[0]) + min(t[1], 4 - t[1]) + 2 * t[2]),
)
CUT_ROWS = 128
HID_CHUNKS = 4
HID_CHUNK = HALF // HID_CHUNKS
OUT_CHUNKS = 4
OUT_CHUNK = WIDTH // OUT_CHUNKS
SCALE = DH**-0.5


def contract_last(left, right):
    return lax.dot_general(left, right, LAST, preferred_element_type=F32)


def dot(left, right):
    return jnp.dot(left, right, preferred_element_type=F32)


def silu(v):
    return v * jax.nn.sigmoid(v)


def silu_slope(v):
    s = jax.nn.sigmoid(v)
    return s * (1.0 + v * (1.0 - s))


def kernel(
    x_hbm, wh_hbm, we_hbm, wq_hbm, wg_hbm, wp_hbm, k_hbm, v_hbm, cut_hbm, cot_hbm,
    out_ref,
    x_v, wh_v, we_v, wq_v, wg_v, wp_v, k_v, v_v, cut_v, cot_v,
    slope_v, hid_slope, enc_send, enc_recv, lin_q, lin_g, gates_v, outg_v, gateg_v, qgrad_v,
    ag, rows_v, sums_v, rs1_send, rs1_recv, rs2_send, rs2_recv,
    emb_send, emb_recv, part_send, part_recv, part_own,
    load_sem, kv_sem, ag_ssem, ag_rsem, rs_ssem, rs_rsem, head_ssem, head_rsem,
):
    xi, yi, zi, ci, hi = (lax.axis_index(a) for a in (*CTX, "head"))
    base = (((xi * 4 + yi) * 2 + zi) * 2 + ci) * EVENTS
    partner = {"head": 1 - hi}
    sibling = {"c": 1 - ci}

    spot = (xi * 4 + yi) * 2 + zi
    peers = []
    for dx, dy, dz in OFFSETS:
        px, py, pz = lax.rem(xi + dx, 4), lax.rem(yi + dy, 4), lax.rem(zi + dz, 2)
        peers.append(((px * 4 + py) * 2 + pz, {"x": px, "y": py, "zh": pz}))

    barrier = pltpu.get_barrier_semaphore()
    for device in [partner, sibling] + [device for _, device in peers]:
        pl.semaphore_signal(barrier, inc=1, device_id=device, device_id_type=pl.DeviceIdType.MESH)

    loads = [pltpu.make_async_copy(x_hbm, x_v, load_sem.at[0])]
    for j in range(HID_CHUNKS):
        cols = pl.ds(j * HID_CHUNK, HID_CHUNK)
        loads.append(
            pltpu.make_async_copy(wh_hbm.at[:, cols], wh_v.at[:, cols], load_sem.at[len(loads)])
        )
    for src, dst in (
        (we_hbm, we_v), (cot_hbm, cot_v), (wp_hbm, wp_v), (wq_hbm, wq_v), (wg_hbm, wg_v),
        (cut_hbm, cut_v),
    ):
        loads.append(pltpu.make_async_copy(src, dst, load_sem.at[len(loads)]))
    for copy in loads:
        copy.start()

    def kv_copies(u):
        return (
            pltpu.make_async_copy(k_hbm.at[u], k_v.at[u], kv_sem.at[0, u]),
            pltpu.make_async_copy(v_hbm.at[u], v_v.at[u], kv_sem.at[1, u]),
        )

    for u in range(USERS):
        for copy in kv_copies(u):
            copy.start()

    loads[0].wait()
    for j in range(HID_CHUNKS):
        loads[1 + j].wait()
        cols = slice(j * HID_CHUNK, (j + 1) * HID_CHUNK)
        lin = dot(x_v[...], wh_v[:, cols])
        s = jax.nn.sigmoid(lin)
        hidden = lin * s
        hid_slope[:, cols] = s * (1.0 + lin * (1.0 - s))
        if j == 0:
            loads[1 + HID_CHUNKS].wait()
        part = dot(hidden.astype(BF), we_v[cols, :])
        total = part if j == 0 else total + part
    enc_send[...] = total[0:32] + total[32:64] + total[64:96] + total[96:128]

    pl.semaphore_wait(barrier, 33)

    def head_copy(src, dst, n):
        return pltpu.make_async_remote_copy(
            src_ref=src, dst_ref=dst, send_sem=head_ssem.at[n], recv_sem=head_rsem.at[n],
            device_id=partner, device_id_type=pl.DeviceIdType.MESH,
        )

    enc_copy = head_copy(enc_send, enc_recv, 0)
    enc_copy.start()
    for n in range(2 + HID_CHUNKS, 7 + HID_CHUNKS):
        loads[n].wait()
    cot = cot_v[...].astype(F32).reshape(OWN, MODEL).astype(BF)
    out_grad = contract_last(cot, wp_v[...]).astype(BF).astype(F32)
    enc_copy.wait()
    embedded = (0.5 * (enc_send[...] + enc_recv[...])).astype(BF)
    query_lin = dot(embedded, wq_v[...])
    lin_q[...] = silu_slope(query_lin)
    queries = silu(query_lin).astype(BF).astype(F32)

    def send(src, dst, ssem, rsem, device):
        pltpu.make_async_remote_copy(
            src_ref=src, dst_ref=dst, send_sem=ssem, recv_sem=rsem,
            device_id=device, device_id_type=pl.DeviceIdType.MESH,
        ).start()

    def whole(ref, ssem, rsem):
        return pltpu.make_async_remote_copy(
            src_ref=ref, dst_ref=ref, send_sem=ssem, recv_sem=rsem,
            device_id=partner, device_id_type=pl.DeviceIdType.MESH,
        )

    def heads_stacked(rows):
        return jnp.concatenate([rows[:, :DH], rows[:, DH:]], axis=0)

    mine = ci * NEAR + spot
    near = pl.ds(ci * NEAR, NEAR)
    far = pl.ds((1 - ci) * NEAR, NEAR)

    def gather_sems(ph, u, n):
        return ag_ssem.at[ph, u, n], ag_rsem.at[ph, u, n]

    def gather_waits(ph, u):
        return (
            whole(ag.at[ph, u, 0 : NEAR - 1], *gather_sems(ph, u, 0)),
            whole(ag.at[ph, u, 0:NEAR], *gather_sems(ph, u, 1)),
        )

    def gather_first(ph, u, block):
        ag[ph, u, mine] = block
        ref = ag.at[ph, u, mine]
        for _, device in peers:
            send(ref, ref, *gather_sems(ph, u, 0), device)

    def gather_last(ph, u):
        gather_waits(ph, u)[0].wait_recv()
        ref = ag.at[ph, u, near]
        send(ref, ref, *gather_sems(ph, u, 1), sibling)

    def gather_end(ph, u):
        gather_waits(ph, u)[1].wait_recv()
        blocks = ag[ph, u].astype(F32)
        for h in range(2):
            rows = blocks[:, h * ROWS : (h + 1) * ROWS, :].reshape(TARGETS, DH)
            rows_v[h] = rows.astype(BF)

    def sum_sems(ph, u, n):
        return rs_ssem.at[ph, u, n], rs_rsem.at[ph, u, n]

    def sum_waits(ph, u):
        return (
            whole(rs1_recv.at[ph, u], *sum_sems(ph, u, 0)),
            whole(rs2_recv.at[ph, u, 0 : NEAR - 1], *sum_sems(ph, u, 1)),
        )

    def sum_first(ph, u):
        rs1_send[ph, u] = sums_v[...].astype(BF)
        send(rs1_send.at[ph, u, far], rs1_recv.at[ph, u], *sum_sems(ph, u, 0), sibling)

    def sum_mid(ph, u):
        sum_waits(ph, u)[0].wait_recv()
        total = rs1_send[ph, u, near].astype(F32) + rs1_recv[ph, u].astype(F32)
        rs2_send[ph, u] = total.astype(BF)
        rs2_recv[ph, u, spot] = rs2_send[ph, u, spot]
        for peer, device in peers:
            send(
                rs2_send.at[ph, u, peer], rs2_recv.at[ph, u, spot], *sum_sems(ph, u, 1), device
            )

    def sum_end(ph, u):
        sum_waits(ph, u)[1].wait_recv()
        return jnp.sum(rs2_recv[ph, u].astype(F32), axis=0)

    for u in range(USERS):
        gather_first(0, u, heads_stacked(queries[u * ROWS : (u + 1) * ROWS]).astype(BF))
    gate_lin = dot(embedded, wg_v[...])
    lin_g[...] = silu_slope(gate_lin)
    gates = silu(gate_lin).astype(BF).astype(F32)
    for u in range(USERS):
        gates_v[u] = heads_stacked(gates[u * ROWS : (u + 1) * ROWS])
        outg_v[u] = heads_stacked(out_grad[u * ROWS : (u + 1) * ROWS])
    gather_last(0, 0)
    gather_last(0, 1)

    def norm_and_gather(u):
        attended = sum_end(0, u)
        grads = outg_v[u]
        rscale = lax.rsqrt(jnp.mean(attended * attended, axis=-1, keepdims=True) + 1e-06)
        normed = attended * rscale
        gateg_v[u] = grads * normed
        ng = grads * gates_v[u]
        grad = rscale * (ng - normed * jnp.mean(ng * normed, axis=-1, keepdims=True))
        gather_first(1, u, grad.astype(BF))

    def query_grad_end(u):
        qgrad_v[u] = sum_end(1, u) * SCALE

    def unstacked(ref):
        return jnp.concatenate(
            [ref[:, h * ROWS : (h + 1) * ROWS, :].reshape(OWN, DH) for h in range(2)], axis=1
        )

    lane = lax.broadcasted_iota(jnp.int32, (1, EVENTS), 1) + base

    def keep(r, h, sums):
        slots = slice(r // ROWS, (r + CUT_ROWS) // ROWS)
        rows = pl.ds(pl.multiple_of(h * ROWS, ROWS), ROWS)
        sums_v[slots, rows, :] = sums.reshape(CUT_ROWS // ROWS, ROWS, DH)

    def forward(u, h):
        cols = pl.ds(pl.multiple_of(h * DH, DH), DH)
        for r in range(0, TARGETS, CUT_ROWS):
            rows = slice(r, r + CUT_ROWS)
            scores = contract_last(rows_v[h, rows, :], k_v[u, :, cols])
            cut = cut_v[u, rows, :]
            visible = lane < jnp.concatenate([cut] * (EVENTS // DH), axis=1)
            y = jnp.where(visible, scores * (0.5 * SCALE), -1e30).astype(BF)
            t = jnp.tanh(y)
            s2 = BF(1) + t
            w = y * s2
            slope_v[u * 2 + h, rows, :] = BF(0.5) * s2 + w * (BF(0.5) - BF(0.5) * t)
            keep(r, h, dot(w, v_v[u, :, cols]))

    def backward(u, h):
        cols = pl.ds(pl.multiple_of(h * DH, DH), DH)
        for r in range(0, TARGETS, CUT_ROWS):
            rows = slice(r, r + CUT_ROWS)
            wgrad = contract_last(rows_v[h, rows, :], v_v[u, :, cols])
            gs = wgrad.astype(BF) * slope_v[u * 2 + h, rows, :]
            keep(r, h, dot(gs, k_v[u, :, cols]))

    @pl.loop(0, 4 * USERS)
    def _(i):
        u = lax.rem(i, 8) // 2
        h = lax.rem(i, 2)

        @pl.when(i < 8)
        def _():
            @pl.when(h == 0)
            def _():
                gather_end(0, u)
                for copy in kv_copies(u):
                    copy.wait()

            forward(u, h)

        @pl.when(i >= 8)
        def _():
            @pl.when(h == 0)
            def _():
                gather_end(1, u)

            backward(u, h)

        @pl.when(h == 1)
        def _():
            sum_first(i // 8, u)

        @pl.when((i == 6) | (i == 7) | (i == 8))
        def _():
            @pl.when(i == 7)
            def _():
                sum_mid(0, 3)

            norm_and_gather(i - 6 + i // 8)

        @pl.when((i == 2) | (i == 4) | (i == 6) | (i == 10) | (i == 12) | (i == 14))
        def _():
            sum_mid(i // 8, lax.rem(i, 8) // 2 - 1)

        @pl.when(i == 7)
        def _():
            gather_last(1, 0)
            norm_and_gather(2)

        @pl.when((i == 8) | (i == 10) | (i == 12))
        def _():
            gather_last(1, i // 2 - 3)

        @pl.when(i == 0)
        def _():
            gather_last(0, 2)
            gather_last(0, 3)

    sum_mid(1, USERS - 1)
    for u in range(USERS):
        query_grad_end(u)

    query_back = (unstacked(qgrad_v) * lin_q[...]).astype(BF)
    gate_back = (unstacked(gateg_v) * lin_g[...]).astype(BF)
    emb_send[...] = (
        contract_last(query_back, wq_v[...]) + contract_last(gate_back, wg_v[...])
    ).astype(BF)
    emb_copy = head_copy(emb_send, emb_recv, 1)
    emb_copy.start()
    emb_copy.wait()
    embed_grad = (0.5 * (emb_send[...].astype(F32) + emb_recv[...].astype(F32))).astype(BF)
    hidden_grad = contract_last(embed_grad, we_v[...])
    hidden_back = jnp.concatenate(
        [(hidden_grad * hid_slope[r * OWN : (r + 1) * OWN, :]).astype(BF) for r in range(EACH)],
        axis=0,
    )
    x_v[...] = hidden_back
    mine = pl.ds(pl.multiple_of(hi * 64, 64), 64)
    other = pl.ds(pl.multiple_of((1 - hi) * 64, 64), 64)
    copies = []
    for j in range(OUT_CHUNKS):
        cols = slice(j * OUT_CHUNK, (j + 1) * OUT_CHUNK)
        part_own[:, cols] = contract_last(x_v[...], wh_v[cols, :])
        part_send[j] = part_own[other, cols].astype(BF)
        copies.append(head_copy(part_send.at[j], part_recv.at[j], 2 + j))
        copies[-1].start()
    for j in range(OUT_CHUNKS):
        cols = slice(j * OUT_CHUNK, (j + 1) * OUT_CHUNK)
        copies[j].wait()
        own = part_own[mine, cols].astype(BF).astype(F32)
        out_ref[:, cols] = (own + part_recv[j].astype(F32)).astype(BF)

    @pl.loop(0, USERS)
    def _(u):
        for ph in range(2):
            for copy in gather_waits(ph, u):
                copy.wait_send()
            for copy in sum_waits(ph, u):
                copy.wait_send()


def body(
    content_rows, w_hidden, w_embed, w_query, w_gate, w_proj,
    history_keys, history_values, cutoffs, out_cotangent,
):
    x = content_rows.transpose(2, 0, 1, 3).reshape(EACH * OWN, WIDTH)
    cut = cutoffs.reshape(USERS, NEAR, 2, ROWS).transpose(0, 2, 1, 3)
    cut = jnp.broadcast_to(cut.reshape(USERS, TARGETS, 1), (USERS, TARGETS, DH))
    dma = pltpu.SemaphoreType.DMA
    v = pltpu.VMEM
    part = pl.pallas_call(
        kernel,
        name="attention_and_encoder",
        out_shape=jax.ShapeDtypeStruct((64, WIDTH), BF),
        in_specs=[pl.BlockSpec(memory_space=pl.ANY)] * 10,
        out_specs=pl.BlockSpec(memory_space=pltpu.VMEM),
        scratch_shapes=[
            v((EACH * OWN, WIDTH), BF), v((WIDTH, HALF), BF), v((HALF, MODEL), BF),
            v((MODEL, LOCAL), BF), v((MODEL, LOCAL), BF), v((LOCAL, MODEL), BF),
            v((USERS, EVENTS, LOCAL), BF), v((USERS, EVENTS, LOCAL), BF),
            v((USERS, TARGETS, DH), jnp.int32), v((USERS, ROWS, MODEL), BF),
            v((2 * USERS, TARGETS, EVENTS), BF), v((EACH * OWN, HALF), F32),
            v((OWN, MODEL), F32), v((OWN, MODEL), F32),
            v((OWN, LOCAL), F32), v((OWN, LOCAL), F32),
            v((USERS, 2 * ROWS, DH), F32), v((USERS, 2 * ROWS, DH), F32),
            v((USERS, 2 * ROWS, DH), F32), v((USERS, 2 * ROWS, DH), F32),
            v((2, USERS, SLOTS, 2 * ROWS, DH), BF), v((2, TARGETS, DH), BF),
            v((SLOTS, 2 * ROWS, DH), F32), v((2, USERS, SLOTS, 2 * ROWS, DH), BF),
            v((2, USERS, NEAR, 2 * ROWS, DH), BF), v((2, USERS, NEAR, 2 * ROWS, DH), BF),
            v((2, USERS, NEAR, 2 * ROWS, DH), BF),
            v((OWN, MODEL), BF), v((OWN, MODEL), BF),
            v((OUT_CHUNKS, 64, OUT_CHUNK), BF), v((OUT_CHUNKS, 64, OUT_CHUNK), BF),
            v((EACH * OWN, WIDTH), F32),
            dma((7 + HID_CHUNKS,)), dma((2, USERS)),
            dma((2, USERS, 2)), dma((2, USERS, 2)), dma((2, USERS, 2)), dma((2, USERS, 2)),
            dma((2 + OUT_CHUNKS,)), dma((2 + OUT_CHUNKS,)),
        ],
        compiler_params=pltpu.CompilerParams(
            collective_id=0, has_side_effects=True, vmem_limit_bytes=62 * 2**20
        ),
    )(
        x, w_hidden, w_embed, w_query, w_gate, w_proj,
        history_keys, history_values, cut, out_cotangent,
    )
    return part.reshape(2, USERS, ROWS, WIDTH).transpose(1, 2, 0, 3)


def solution(mesh):
    split = Mesh(
        mesh.devices.reshape(4, 4, 2, 2, mesh.shape["head"]),
        (*CTX, "head"),
    )
    return jax.shard_map(
        body,
        mesh=split,
        in_specs=(
            P(None, CTX, None, None), P(None, "head"), P("head", None), P(None, "head"),
            P(None, "head"), P("head", None), P(None, CTX, "head"), P(None, CTX, "head"),
            P(), P(None, CTX, None),
        ),
        out_specs=P(None, CTX, "head", None),
        check_vma=False,
    )
```

time: 114 us -> 87.9 us (0.77)
  Pallas kernels: 108 us -> 81.2 us
    pallas_call x1, Pallas kernels: 108 us -> 81.2 us  [body(): pl.pallas_call(kernel, name='attention_and_encoder', out_shape=jax.ShapeD...]
where the time goes in v2:
time: 87.9 us; the launch traced here: 87.7 us
  Pallas kernels  81.2 us (92%)
  local copies, waits for them, and re-layouts  6.46 us (7%)
    pallas_call x1, Pallas kernels, body(): pl.pallas_call(kernel, name='attention_and_encoder', out_shape=jax.ShapeD...  81.2 us
    transpose x1, local copies, waits for them, and re-layouts, body(): x = content_rows.transpose(2, 0, 1, 3).reshape(EACH * OWN, WIDTH)  2.15 us
    reshape x1, local copies, waits for them, and re-layouts, body(): return part.reshape(2, USERS, ROWS, WIDTH).transpose(1, 2, 0, 3)  1.92 us

profile of v2, /device:TPU:0, one launch (start us, length us, event | category | flops | bytes accessed | tf_op | source)
XLA Modules:
  0.0 87.7 jit_solution(17049494660498091472)
XLA Ops:
  0.0 0.9 %reshape.12 = s32[4,32,2,8]{3,2,1,0:T(2,128)S(1)} reshape(s32[4,512]{1,0:T(4,128)} %param.18) | data formatting | bytes 16384 | tf_op jit(solution)/shard_map/reshape | solution.py:362
  1.0 0.1 broadcast_in_dim.7
  1.1 2.2 %copy.14 = bf16[4,4,8,2048]{3,2,1,0:T(8,128)(2,1)} copy(bf16[4,4,8,2048]{3,0,2,1:T(4,128)(2,1)} %bitcast.11) | data formatting | bytes 1048576 | tf_op jit(solution)/shard_map/transpose | solution.py:361
  3.2 1.3 %broadcast_in_dim.8.cut_hbm = s32[4,512,128]{2,1,0:T(8,128)} broadcast(s32[4,512]{1,0:T(4,128)S(1)} %broadcast_in_dim.7), dimensions={0,1} | broadcast | bytes 1056768 | tf_op jit(solution)/shard_map/broadcast_in_dim | solution.py:363
  4.6 81.2 %attention_and_encoder.1 = bf16[64,2048]{1,0:T(8,128)(2,1)} custom-call(bf16[128,2048]{1,0:T(8,128)(2,1)} %bitcast.9, bf16[2048,2048]{1,0:T(8,128)(2,1)} %wh_hbm.1, bf16[2048,512]{1,0:T(8,128)(2,1)} %we_hbm.1, bf16[512,256]{1,0:T(8,128)(2,1)} %wq_hbm.1, bf16[512,256]{1,0:T(8,128)(2,1)} %wg_hbm.1, bf16[256,512]{1,0:T(8,128)(2,1)} %wp_hbm.1, ...), custom_call_target="tpu_custom_call" | custom-call | tf_op jit(solution)/shard_map/attention_and_encoder/pallas_call | solution.py:366
  85.7 1.9 %copy.18 = bf16[2,4,8,2048]{3,0,2,1:T(2,128)(2,1)} copy(bf16[2,4,8,2048]{3,2,1,0:T(8,128)(2,1)} %bitcast.10) | data formatting | bytes 524288 | tf_op jit(solution)/shard_map/reshape | solution.py:400
  (1 shorter events, 0.0 us)

commit v3 on v2

--- a/solution.py
+++ b/solution.py
@@ -48,7 +48,7 @@
 def kernel(
     x_hbm, wh_hbm, we_hbm, wq_hbm, wg_hbm, wp_hbm, k_hbm, v_hbm, cut_hbm, cot_hbm,
     out_ref,
-    x_v, wh_v, we_v, wq_v, wg_v, wp_v, k_v, v_v, cut_v, cot_v,
+    x_in, cut_in, pairs_v, x_v, wh_v, we_v, wq_v, wg_v, wp_v, k_v, v_v, cut_v, cot_v,
     slope_v, hid_slope, enc_send, enc_recv, lin_q, lin_g, gates_v, outg_v, gateg_v, qgrad_v,
     ag, rows_v, sums_v, rs1_send, rs1_recv, rs2_send, rs2_recv,
     emb_send, emb_recv, part_send, part_recv, part_own,
@@ -65,11 +65,7 @@
         px, py, pz = lax.rem(xi + dx, 4), lax.rem(yi + dy, 4), lax.rem(zi + dz, 2)
         peers.append(((px * 4 + py) * 2 + pz, {"x": px, "y": py, "zh": pz}))
 
-    barrier = pltpu.get_barrier_semaphore()
-    for device in [partner, sibling] + [device for _, device in peers]:
-        pl.semaphore_signal(barrier, inc=1, device_id=device, device_id_type=pl.DeviceIdType.MESH)
-
-    loads = [pltpu.make_async_copy(x_hbm, x_v, load_sem.at[0])]
+    loads = [pltpu.make_async_copy(x_hbm, x_in, load_sem.at[0])]
     for j in range(HID_CHUNKS):
         cols = pl.ds(j * HID_CHUNK, HID_CHUNK)
         loads.append(
@@ -77,7 +73,7 @@
         )
     for src, dst in (
         (we_hbm, we_v), (cot_hbm, cot_v), (wp_hbm, wp_v), (wq_hbm, wq_v), (wg_hbm, wg_v),
-        (cut_hbm, cut_v),
+        (cut_hbm, cut_in),
     ):
         loads.append(pltpu.make_async_copy(src, dst, load_sem.at[len(loads)]))
     for copy in loads:
@@ -89,11 +85,18 @@
             pltpu.make_async_copy(v_hbm.at[u], v_v.at[u], kv_sem.at[1, u]),
         )
 
-    for u in range(USERS):
-        for copy in kv_copies(u):
-            copy.start()
-
+    barrier = pltpu.get_barrier_semaphore()
+    for device in [partner, sibling] + [device for _, device in peers]:
+        pl.semaphore_signal(barrier, inc=1, device_id=device, device_id_type=pl.DeviceIdType.MESH)
+
+    row = lax.broadcasted_iota(jnp.int32, (EACH * OWN, EACH * OWN), 0)
+    col = lax.broadcasted_iota(jnp.int32, (EACH * OWN, EACH * OWN), 1)
+    target = (row % 64) // 2
+    picked = col == target * EACH + (row // 64) * 2 + row % 2
+    order = jnp.where(picked, 1.0, 0.0).astype(BF)
+    spread = jnp.where(target == col, 1.0, 0.0)[:, :OWN].astype(BF)
     loads[0].wait()
+    x_v[...] = dot(order, x_in[...].reshape(EACH * OWN, WIDTH)).astype(BF)
     for j in range(HID_CHUNKS):
         loads[1 + j].wait()
         cols = slice(j * HID_CHUNK, (j + 1) * HID_CHUNK)
@@ -105,7 +108,17 @@
             loads[1 + HID_CHUNKS].wait()
         part = dot(hidden.astype(BF), we_v[cols, :])
         total = part if j == 0 else total + part
-    enc_send[...] = total[0:32] + total[32:64] + total[64:96] + total[96:128]
+    for u in range(USERS):
+        for copy in kv_copies(u):
+            copy.start()
+    for n in range(2 + HID_CHUNKS, 7 + HID_CHUNKS):
+        loads[n].wait()
+    pairs = total[0:64] + total[64:128]
+    for n in range(MODEL // DH):
+        cols = slice(n * DH, (n + 1) * DH)
+        pairs_v[n] = pairs[:, cols]
+        even, odd = (pairs_v[n, pl.ds(k, OWN, stride=2), :] for k in range(2))
+        enc_send[:, cols] = even + odd
 
     pl.semaphore_wait(barrier, 33)
 
@@ -117,8 +130,12 @@
 
     enc_copy = head_copy(enc_send, enc_recv, 0)
     enc_copy.start()
-    for n in range(2 + HID_CHUNKS, 7 + HID_CHUNKS):
-        loads[n].wait()
+    for u in range(USERS):
+        limits = jnp.clip(cut_in[u : u + 1, :] - base, 0, EVENTS)
+        limits = jnp.broadcast_to(limits, (DH, TARGETS)).T.reshape(NEAR, 2 * ROWS, DH)
+        for n in range(2):
+            part = limits[:, n * ROWS : (n + 1) * ROWS, :].reshape(TARGETS // 2, DH)
+            cut_v[u, n * (TARGETS // 2) : (n + 1) * (TARGETS // 2), :] = part.astype(jnp.int16)
     cot = cot_v[...].astype(F32).reshape(OWN, MODEL).astype(BF)
     out_grad = contract_last(cot, wp_v[...]).astype(BF).astype(F32)
     enc_copy.wait()
@@ -222,14 +239,15 @@
         gather_first(1, u, grad.astype(BF))
 
     def query_grad_end(u):
-        qgrad_v[u] = sum_end(1, u) * SCALE
+        qgrad_v[u] = sum_end(1, u) * (0.5 * SCALE)
 
     def unstacked(ref):
         return jnp.concatenate(
             [ref[:, h * ROWS : (h + 1) * ROWS, :].reshape(OWN, DH) for h in range(2)], axis=1
         )
 
-    lane = lax.broadcasted_iota(jnp.int32, (1, EVENTS), 1) + base
+    lane = lax.broadcasted_iota(jnp.int32, (2 * ROWS, EVENTS), 1).astype(jnp.int16)
+    lane = jnp.concatenate([lane] * (CUT_ROWS // (2 * ROWS)), axis=0)
 
     def keep(r, h, sums):
         slots = slice(r // ROWS, (r + CUT_ROWS) // ROWS)
@@ -243,11 +261,11 @@
             scores = contract_last(rows_v[h, rows, :], k_v[u, :, cols])
             cut = cut_v[u, rows, :]
             visible = lane < jnp.concatenate([cut] * (EVENTS // DH), axis=1)
-            y = jnp.where(visible, scores * (0.5 * SCALE), -1e30).astype(BF)
-            t = jnp.tanh(y)
+            y = (scores * (0.5 * SCALE)).astype(BF)
+            t = jnp.where(visible, jnp.tanh(y), BF(-1))
             s2 = BF(1) + t
             w = y * s2
-            slope_v[u * 2 + h, rows, :] = BF(0.5) * s2 + w * (BF(0.5) - BF(0.5) * t)
+            slope_v[u * 2 + h, rows, :] = s2 + w * (BF(1) - t)
             keep(r, h, dot(w, v_v[u, :, cols]))
 
     def backward(u, h):
@@ -324,12 +342,8 @@
     emb_copy.start()
     emb_copy.wait()
     embed_grad = (0.5 * (emb_send[...].astype(F32) + emb_recv[...].astype(F32))).astype(BF)
-    hidden_grad = contract_last(embed_grad, we_v[...])
-    hidden_back = jnp.concatenate(
-        [(hidden_grad * hid_slope[r * OWN : (r + 1) * OWN, :]).astype(BF) for r in range(EACH)],
-        axis=0,
-    )
-    x_v[...] = hidden_back
+    hidden_grad = contract_last(dot(spread, embed_grad).astype(BF), we_v[...])
+    x_v[...] = (hidden_grad * hid_slope[...]).astype(BF)
     mine = pl.ds(pl.multiple_of(hi * 64, 64), 64)
     other = pl.ds(pl.multiple_of((1 - hi) * 64, 64), 64)
     copies = []
@@ -358,9 +372,6 @@
     content_rows, w_hidden, w_embed, w_query, w_gate, w_proj,
     history_keys, history_values, cutoffs, out_cotangent,
 ):
-    x = content_rows.transpose(2, 0, 1, 3).reshape(EACH * OWN, WIDTH)
-    cut = cutoffs.reshape(USERS, NEAR, 2, ROWS).transpose(0, 2, 1, 3)
-    cut = jnp.broadcast_to(cut.reshape(USERS, TARGETS, 1), (USERS, TARGETS, DH))
     dma = pltpu.SemaphoreType.DMA
     v = pltpu.VMEM
     part = pl.pallas_call(
@@ -370,10 +381,11 @@
         in_specs=[pl.BlockSpec(memory_space=pl.ANY)] * 10,
         out_specs=pl.BlockSpec(memory_space=pltpu.VMEM),
         scratch_shapes=[
+            v((USERS, ROWS, EACH, WIDTH), BF), v((USERS, TARGETS), jnp.int32), v((MODEL // DH, 64, DH), F32),
             v((EACH * OWN, WIDTH), BF), v((WIDTH, HALF), BF), v((HALF, MODEL), BF),
             v((MODEL, LOCAL), BF), v((MODEL, LOCAL), BF), v((LOCAL, MODEL), BF),
             v((USERS, EVENTS, LOCAL), BF), v((USERS, EVENTS, LOCAL), BF),
-            v((USERS, TARGETS, DH), jnp.int32), v((USERS, ROWS, MODEL), BF),
+            v((USERS, TARGETS, DH), jnp.int16), v((USERS, ROWS, MODEL), BF),
             v((2 * USERS, TARGETS, EVENTS), BF), v((EACH * OWN, HALF), F32),
             v((OWN, MODEL), F32), v((OWN, MODEL), F32),
             v((OWN, LOCAL), F32), v((OWN, LOCAL), F32),
@@ -394,10 +406,10 @@
             collective_id=0, has_side_effects=True, vmem_limit_bytes=62 * 2**20
         ),
     )(
-        x, w_hidden, w_embed, w_query, w_gate, w_proj,
-        history_keys, history_values, cut, out_cotangent,
+        content_rows, w_hidden, w_embed, w_query, w_gate, w_proj,
+        history_keys, history_values, cutoffs, out_cotangent,
     )
-    return part.reshape(2, USERS, ROWS, WIDTH).transpose(1, 2, 0, 3)
+    return part.reshape(USERS, ROWS, 2, WIDTH)
 
 
 def solution(mesh):

time: 87.9 us -> 81.2 us (0.924)
  local copies, waits for them, and re-layouts: 6.46 us -> 1.84 us
  Pallas kernels: 81.2 us -> 79.3 us
    transpose x2 -> x0, local copies, waits for them, and re-layouts: 2.16 us -> none  [the longest x1 2.15 us: body(): x = content_rows.transpose(2, 0, 1, 3).reshape(EACH * OWN, WIDTH)]
    pallas_call x1, Pallas kernels: 81.2 us -> 79.3 us  [body(): pl.pallas_call(kernel, name='attention_and_encoder', out_shape=jax.ShapeD...]
    broadcast_in_dim x2 -> x0, local copies, waits for them, and re-layouts: 1.44 us -> none  [body(): cut = jnp.broadcast_to(cut.reshape(USERS, TARGETS, 1), (USERS, TARGETS, DH))]
    reshape x2 -> x1, local copies, waits for them, and re-layouts: 2.85 us -> 1.84 us  [body(): return part.reshape(USERS, ROWS, 2, WIDTH)]
where the time goes in v3:
time: 81.2 us; the launch traced here: 81.1 us
  Pallas kernels  79.3 us (98%)
  local copies, waits for them, and re-layouts  1.84 us (2%)
    pallas_call x1, Pallas kernels, body(): pl.pallas_call(kernel, name='attention_and_encoder', out_shape=jax.ShapeD...  79.3 us
    reshape x1, local copies, waits for them, and re-layouts, body(): return part.reshape(USERS, ROWS, 2, WIDTH)  1.84 us

profile of v3, /device:TPU:0, one launch (start us, length us, event | category | flops | bytes accessed | tf_op | source)
XLA Modules:
  0.0 81.1 jit_solution(5478941155271358006)
XLA Ops:
  0.0 79.3 %attention_and_encoder.1 = bf16[64,2048]{1,0:T(8,128)(2,1)} custom-call(bf16[4,8,4,2048]{3,2,1,0:T(4,128)(2,1)} %x_hbm.1, bf16[2048,2048]{1,0:T(8,128)(2,1)} %wh_hbm.1, bf16[2048,512]{1,0:T(8,128)(2,1)} %we_hbm.1, bf16[512,256]{1,0:T(8,128)(2,1)} %wq_hbm.1, bf16[512,256]{1,0:T(8,128)(2,1)} %wg_hbm.1, bf16[256,512]{1,0:T(8,128)(2,1)} %wp_hbm.1, ...), custom_call_target="tpu_custom_call" | custom-call | tf_op jit(solution)/shard_map/attention_and_encoder/pallas_call | solution.py:377
  79.3 1.8 %reshape.3 = bf16[4,8,2,2048]{3,2,1,0:T(2,128)(2,1)} reshape(bf16[64,2048]{1,0:T(8,128)(2,1)} %attention_and_encoder.1) | data formatting | bytes 524288 | tf_op jit(solution)/shard_map/reshape | solution.py:412

commit v4 on v3

--- a/solution.py
+++ b/solution.py
@@ -15,12 +15,12 @@
 HALF, MODEL, LOCAL = 2048, 512, 256
 TARGETS, EVENTS = 512, 2304
 OWN = USERS * ROWS
+GROUP = 2 * ROWS
 SLOTS, NEAR = 64, 32
 OFFSETS = sorted(
     [(a, b, c) for a in range(4) for b in range(4) for c in range(2) if a or b or c],
     key=lambda t: -(min(t[0], 4 - t[0]) + min(t[1], 4 - t[1]) + 2 * t[2]),
 )
-CUT_ROWS = 128
 HID_CHUNKS = 4
 HID_CHUNK = HALF // HID_CHUNKS
 OUT_CHUNKS = 4
@@ -30,6 +30,10 @@
 
 def contract_last(left, right):
     return lax.dot_general(left, right, LAST, preferred_element_type=F32)
+
+
+def contract_first(left, right):
+    return lax.dot_general(left, right, (((0,), (0,)), ((), ())), preferred_element_type=F32)
 
 
 def dot(left, right):
@@ -65,6 +69,10 @@
         px, py, pz = lax.rem(xi + dx, 4), lax.rem(yi + dy, 4), lax.rem(zi + dz, 2)
         peers.append(((px * 4 + py) * 2 + pz, {"x": px, "y": py, "zh": pz}))
 
+    barrier = pltpu.get_barrier_semaphore()
+    for device in [partner, sibling] + [device for _, device in peers]:
+        pl.semaphore_signal(barrier, inc=1, device_id=device, device_id_type=pl.DeviceIdType.MESH)
+
     loads = [pltpu.make_async_copy(x_hbm, x_in, load_sem.at[0])]
     for j in range(HID_CHUNKS):
         cols = pl.ds(j * HID_CHUNK, HID_CHUNK)
@@ -85,14 +93,10 @@
             pltpu.make_async_copy(v_hbm.at[u], v_v.at[u], kv_sem.at[1, u]),
         )
 
-    barrier = pltpu.get_barrier_semaphore()
-    for device in [partner, sibling] + [device for _, device in peers]:
-        pl.semaphore_signal(barrier, inc=1, device_id=device, device_id_type=pl.DeviceIdType.MESH)
-
     row = lax.broadcasted_iota(jnp.int32, (EACH * OWN, EACH * OWN), 0)
     col = lax.broadcasted_iota(jnp.int32, (EACH * OWN, EACH * OWN), 1)
-    target = (row % 64) // 2
-    picked = col == target * EACH + (row // 64) * 2 + row % 2
+    target = (row // 64) * GROUP + (row % 32) // 2
+    picked = col == target * EACH + ((row % 64) // 32) * 2 + row % 2
     order = jnp.where(picked, 1.0, 0.0).astype(BF)
     spread = jnp.where(target == col, 1.0, 0.0)[:, :OWN].astype(BF)
     loads[0].wait()
@@ -113,7 +117,7 @@
             copy.start()
     for n in range(2 + HID_CHUNKS, 7 + HID_CHUNKS):
         loads[n].wait()
-    pairs = total[0:64] + total[64:128]
+    pairs = jnp.concatenate([total[0:32] + total[32:64], total[64:96] + total[96:128]], axis=0)
     for n in range(MODEL // DH):
         cols = slice(n * DH, (n + 1) * DH)
         pairs_v[n] = pairs[:, cols]
@@ -133,9 +137,8 @@
     for u in range(USERS):
         limits = jnp.clip(cut_in[u : u + 1, :] - base, 0, EVENTS)
         limits = jnp.broadcast_to(limits, (DH, TARGETS)).T.reshape(NEAR, 2 * ROWS, DH)
-        for n in range(2):
-            part = limits[:, n * ROWS : (n + 1) * ROWS, :].reshape(TARGETS // 2, DH)
-            cut_v[u, n * (TARGETS // 2) : (n + 1) * (TARGETS // 2), :] = part.astype(jnp.int16)
+        halves = [limits[:, n * ROWS : (n + 1) * ROWS, :].reshape(TARGETS // 2, DH) for n in range(2)]
+        cut_v[u] = jnp.concatenate(halves, axis=0).T[: 2 * ROWS, :].astype(jnp.int16)
     cot = cot_v[...].astype(F32).reshape(OWN, MODEL).astype(BF)
     out_grad = contract_last(cot, wp_v[...]).astype(BF).astype(F32)
     enc_copy.wait()
@@ -241,40 +244,31 @@
     def query_grad_end(u):
         qgrad_v[u] = sum_end(1, u) * (0.5 * SCALE)
 
-    def unstacked(ref):
-        return jnp.concatenate(
-            [ref[:, h * ROWS : (h + 1) * ROWS, :].reshape(OWN, DH) for h in range(2)], axis=1
-        )
-
-    lane = lax.broadcasted_iota(jnp.int32, (2 * ROWS, EVENTS), 1).astype(jnp.int16)
-    lane = jnp.concatenate([lane] * (CUT_ROWS // (2 * ROWS)), axis=0)
-
-    def keep(r, h, sums):
-        slots = slice(r // ROWS, (r + CUT_ROWS) // ROWS)
+    def unstacked(ref, g):
+        blocks = [ref[2 * g : 2 * g + 2, h * ROWS : (h + 1) * ROWS, :] for h in range(2)]
+        return jnp.concatenate([block.reshape(GROUP, DH) for block in blocks], axis=1)
+
+    def keep(h, sums):
         rows = pl.ds(pl.multiple_of(h * ROWS, ROWS), ROWS)
-        sums_v[slots, rows, :] = sums.reshape(CUT_ROWS // ROWS, ROWS, DH)
+        sums_v[:, rows, :] = sums.T.reshape(SLOTS, ROWS, DH)
 
     def forward(u, h):
         cols = pl.ds(pl.multiple_of(h * DH, DH), DH)
-        for r in range(0, TARGETS, CUT_ROWS):
-            rows = slice(r, r + CUT_ROWS)
-            scores = contract_last(rows_v[h, rows, :], k_v[u, :, cols])
-            cut = cut_v[u, rows, :]
-            visible = lane < jnp.concatenate([cut] * (EVENTS // DH), axis=1)
-            y = (scores * (0.5 * SCALE)).astype(BF)
-            t = jnp.where(visible, jnp.tanh(y), BF(-1))
-            s2 = BF(1) + t
-            w = y * s2
-            slope_v[u * 2 + h, rows, :] = s2 + w * (BF(1) - t)
-            keep(r, h, dot(w, v_v[u, :, cols]))
+        scores = contract_last(k_v[u, :, cols], rows_v[h])
+        place = lax.broadcasted_iota(jnp.int32, (EVENTS, TARGETS), 0).astype(jnp.int16)
+        visible = place < jnp.concatenate([cut_v[u]] * (EVENTS // (2 * ROWS)), axis=0)
+        y = (scores * (0.5 * SCALE)).astype(BF)
+        t = jnp.where(visible, jnp.tanh(y), BF(-1))
+        s2 = BF(1) + t
+        w = y * s2
+        slope_v[u * 2 + h] = s2 + w * (BF(1) - t)
+        keep(h, contract_first(v_v[u, :, cols], w))
 
     def backward(u, h):
         cols = pl.ds(pl.multiple_of(h * DH, DH), DH)
-        for r in range(0, TARGETS, CUT_ROWS):
-            rows = slice(r, r + CUT_ROWS)
-            wgrad = contract_last(rows_v[h, rows, :], v_v[u, :, cols])
-            gs = wgrad.astype(BF) * slope_v[u * 2 + h, rows, :]
-            keep(r, h, dot(gs, k_v[u, :, cols]))
+        wgrad = contract_last(v_v[u, :, cols], rows_v[h])
+        gs = wgrad.astype(BF) * slope_v[u * 2 + h]
+        keep(h, contract_first(k_v[u, :, cols], gs))
 
     @pl.loop(0, 4 * USERS)
     def _(i):
@@ -330,34 +324,52 @@
             gather_last(0, 3)
 
     sum_mid(1, USERS - 1)
-    for u in range(USERS):
-        query_grad_end(u)
-
-    query_back = (unstacked(qgrad_v) * lin_q[...]).astype(BF)
-    gate_back = (unstacked(gateg_v) * lin_g[...]).astype(BF)
-    emb_send[...] = (
-        contract_last(query_back, wq_v[...]) + contract_last(gate_back, wg_v[...])
-    ).astype(BF)
-    emb_copy = head_copy(emb_send, emb_recv, 1)
-    emb_copy.start()
-    emb_copy.wait()
-    embed_grad = (0.5 * (emb_send[...].astype(F32) + emb_recv[...].astype(F32))).astype(BF)
-    hidden_grad = contract_last(dot(spread, embed_grad).astype(BF), we_v[...])
-    x_v[...] = (hidden_grad * hid_slope[...]).astype(BF)
-    mine = pl.ds(pl.multiple_of(hi * 64, 64), 64)
-    other = pl.ds(pl.multiple_of((1 - hi) * 64, 64), 64)
-    copies = []
-    for j in range(OUT_CHUNKS):
-        cols = slice(j * OUT_CHUNK, (j + 1) * OUT_CHUNK)
-        part_own[:, cols] = contract_last(x_v[...], wh_v[cols, :])
-        part_send[j] = part_own[other, cols].astype(BF)
-        copies.append(head_copy(part_send.at[j], part_recv.at[j], 2 + j))
-        copies[-1].start()
-    for j in range(OUT_CHUNKS):
-        cols = slice(j * OUT_CHUNK, (j + 1) * OUT_CHUNK)
-        copies[j].wait()
-        own = part_own[mine, cols].astype(BF).astype(F32)
-        out_ref[:, cols] = (own + part_recv[j].astype(F32)).astype(BF)
+
+    emb_copies, part_copies = [], []
+
+    def embed_part(g):
+        rows = slice(g * GROUP, (g + 1) * GROUP)
+        for u in (2 * g, 2 * g + 1):
+            query_grad_end(u)
+        query_back = (unstacked(qgrad_v, g) * lin_q[rows, :]).astype(BF)
+        gate_back = (unstacked(gateg_v, g) * lin_g[rows, :]).astype(BF)
+        emb_send[g] = (
+            contract_last(query_back, wq_v[...]) + contract_last(gate_back, wg_v[...])
+        ).astype(BF)
+        emb_copies.append(head_copy(emb_send.at[g], emb_recv.at[g], 1 + g))
+        emb_copies[g].start()
+
+    def content_part(g):
+        emb_copies[g].wait()
+        embed_grad = (0.5 * (emb_send[g].astype(F32) + emb_recv[g].astype(F32))).astype(BF)
+        rows = slice(g * 64, (g + 1) * 64)
+        spread_here = spread[rows, g * GROUP : (g + 1) * GROUP]
+        hidden_grad = contract_last(dot(spread_here, embed_grad).astype(BF), we_v[...])
+        x_v[rows, :] = (hidden_grad * hid_slope[rows, :]).astype(BF)
+        other = pl.ds(pl.multiple_of((1 - hi) * 32, 32), 32)
+        for j in range(OUT_CHUNKS):
+            cols = slice(j * OUT_CHUNK, (j + 1) * OUT_CHUNK)
+            part_own[g, :, cols] = contract_last(x_v[rows, :], wh_v[cols, :])
+            part_send[g, j] = part_own[g, other, cols].astype(BF)
+            n = g * OUT_CHUNKS + j
+            part_copies.append(head_copy(part_send.at[g, j], part_recv.at[g, j], 3 + n))
+            part_copies[n].start()
+
+    def content_end(g):
+        mine = pl.ds(pl.multiple_of(hi * 32, 32), 32)
+        for j in range(OUT_CHUNKS):
+            cols = slice(j * OUT_CHUNK, (j + 1) * OUT_CHUNK)
+            part_copies[g * OUT_CHUNKS + j].wait()
+            own = part_own[g, mine, cols].astype(BF).astype(F32)
+            total = (own + part_recv[g, j].astype(F32)).astype(BF)
+            out_ref[2 * g : 2 * g + 2, :, :, cols] = total.reshape(2, ROWS, 2, OUT_CHUNK)
+
+    embed_part(0)
+    content_part(0)
+    embed_part(1)
+    content_end(0)
+    content_part(1)
+    content_end(1)
 
     @pl.loop(0, USERS)
     def _(u):
@@ -377,7 +389,7 @@
     part = pl.pallas_call(
         kernel,
         name="attention_and_encoder",
-        out_shape=jax.ShapeDtypeStruct((64, WIDTH), BF),
+        out_shape=jax.ShapeDtypeStruct((USERS, ROWS, 2, WIDTH), BF),
         in_specs=[pl.BlockSpec(memory_space=pl.ANY)] * 10,
         out_specs=pl.BlockSpec(memory_space=pltpu.VMEM),
         scratch_shapes=[
@@ -385,8 +397,8 @@
             v((EACH * OWN, WIDTH), BF), v((WIDTH, HALF), BF), v((HALF, MODEL), BF),
             v((MODEL, LOCAL), BF), v((MODEL, LOCAL), BF), v((LOCAL, MODEL), BF),
             v((USERS, EVENTS, LOCAL), BF), v((USERS, EVENTS, LOCAL), BF),
-            v((USERS, TARGETS, DH), jnp.int16), v((USERS, ROWS, MODEL), BF),
-            v((2 * USERS, TARGETS, EVENTS), BF), v((EACH * OWN, HALF), F32),
+            v((USERS, 2 * ROWS, TARGETS), jnp.int16), v((USERS, ROWS, MODEL), BF),
+            v((2 * USERS, EVENTS, TARGETS), BF), v((EACH * OWN, HALF), F32),
             v((OWN, MODEL), F32), v((OWN, MODEL), F32),
             v((OWN, LOCAL), F32), v((OWN, LOCAL), F32),
             v((USERS, 2 * ROWS, DH), F32), v((USERS, 2 * ROWS, DH), F32),
@@ -395,12 +407,12 @@
             v((SLOTS, 2 * ROWS, DH), F32), v((2, USERS, SLOTS, 2 * ROWS, DH), BF),
             v((2, USERS, NEAR, 2 * ROWS, DH), BF), v((2, USERS, NEAR, 2 * ROWS, DH), BF),
             v((2, USERS, NEAR, 2 * ROWS, DH), BF),
-            v((OWN, MODEL), BF), v((OWN, MODEL), BF),
-            v((OUT_CHUNKS, 64, OUT_CHUNK), BF), v((OUT_CHUNKS, 64, OUT_CHUNK), BF),
-            v((EACH * OWN, WIDTH), F32),
+            v((2, GROUP, MODEL), BF), v((2, GROUP, MODEL), BF),
+            v((2, OUT_CHUNKS, 32, OUT_CHUNK), BF), v((2, OUT_CHUNKS, 32, OUT_CHUNK), BF),
+            v((2, 64, WIDTH), F32),
             dma((7 + HID_CHUNKS,)), dma((2, USERS)),
             dma((2, USERS, 2)), dma((2, USERS, 2)), dma((2, USERS, 2)), dma((2, USERS, 2)),
-            dma((2 + OUT_CHUNKS,)), dma((2 + OUT_CHUNKS,)),
+            dma((3 + 2 * OUT_CHUNKS,)), dma((3 + 2 * OUT_CHUNKS,)),
         ],
         compiler_params=pltpu.CompilerParams(
             collective_id=0, has_side_effects=True, vmem_limit_bytes=62 * 2**20
@@ -409,7 +421,7 @@
         content_rows, w_hidden, w_embed, w_query, w_gate, w_proj,
         history_keys, history_values, cutoffs, out_cotangent,
     )
-    return part.reshape(USERS, ROWS, 2, WIDTH)
+    return part
 
 
 def solution(mesh):

time: 81.2 us -> 78.2 us (0.963)
  Pallas kernels: 79.3 us -> 76 us
    pallas_call x1, Pallas kernels: 79.3 us -> 76 us  [body(): pl.pallas_call(kernel, name='attention_and_encoder', out_shape=jax.ShapeD...]
    unnamed x0 -> x1, local copies, waits for them, and re-layouts: none -> 1.85 us
    reshape x1 -> x0, local copies, waits for them, and re-layouts: 1.84 us -> none  [body(): return part.reshape(USERS, ROWS, 2, WIDTH)]
where the time goes in v4:
time: 78.2 us; the launch traced here: 77.9 us
  Pallas kernels  76 us (97%)
  local copies, waits for them, and re-layouts  1.85 us (2%)
    pallas_call x1, Pallas kernels, body(): pl.pallas_call(kernel, name='attention_and_encoder', out_shape=jax.ShapeD...  76 us
    unnamed x1, local copies, waits for them, and re-layouts  1.85 us

profile of v4, /device:TPU:0, one launch (start us, length us, event | category | flops | bytes accessed | tf_op | source)
XLA Modules:
  0.0 77.9 jit_solution(9117890087063543218)
XLA Ops:
  0.0 76.0 %attention_and_encoder.1 = bf16[4,8,2,2048]{3,2,1,0:T(2,128)(2,1)} custom-call(bf16[4,8,4,2048]{3,2,1,0:T(4,128)(2,1)} %x_hbm.1, bf16[2048,2048]{1,0:T(8,128)(2,1)} %wh_hbm.1, bf16[2048,512]{1,0:T(8,128)(2,1)} %we_hbm.1, bf16[512,256]{1,0:T(8,128)(2,1)} %wq_hbm.1, bf16[512,256]{1,0:T(8,128)(2,1)} %wg_hbm.1, bf16[256,512]{1,0:T(8,128)(2,1)} %wp_hbm.1, ...), custom_call_target="tpu_custom_call" | custom-call | tf_op jit(solution)/shard_map/attention_and_encoder/pallas_call | solution.py:389
  76.0 1.8 %copy.12 = bf16[4,8,2,2048]{3,2,1,0:T(2,128)(2,1)} copy(bf16[4,8,2,2048]{3,2,1,0:T(2,128)(2,1)} %attention_and_encoder.1) | data formatting | bytes 524288

commit v5 on v4

--- a/solution.py
+++ b/solution.py
@@ -144,7 +144,6 @@
     enc_copy.wait()
     embedded = (0.5 * (enc_send[...] + enc_recv[...])).astype(BF)
     query_lin = dot(embedded, wq_v[...])
-    lin_q[...] = silu_slope(query_lin)
     queries = silu(query_lin).astype(BF).astype(F32)
 
     def send(src, dst, ssem, rsem, device):
@@ -220,8 +219,10 @@
         sum_waits(ph, u)[1].wait_recv()
         return jnp.sum(rs2_recv[ph, u].astype(F32), axis=0)
 
-    for u in range(USERS):
-        gather_first(0, u, heads_stacked(queries[u * ROWS : (u + 1) * ROWS]).astype(BF))
+    blocks = [heads_stacked(queries[u * ROWS : (u + 1) * ROWS]).astype(BF) for u in range(USERS)]
+    for u in range(2):
+        gather_first(0, u, blocks[u])
+    lin_q[...] = silu_slope(query_lin)
     gate_lin = dot(embedded, wg_v[...])
     lin_g[...] = silu_slope(gate_lin)
     gates = silu(gate_lin).astype(BF).astype(F32)
@@ -229,6 +230,8 @@
         gates_v[u] = heads_stacked(gates[u * ROWS : (u + 1) * ROWS])
         outg_v[u] = heads_stacked(out_grad[u * ROWS : (u + 1) * ROWS])
     gather_last(0, 0)
+    for u in range(2, USERS):
+        gather_first(0, u, blocks[u])
     gather_last(0, 1)
 
     def norm_and_gather(u):
@@ -318,7 +321,7 @@
         def _():
             gather_last(1, i // 2 - 3)
 
-        @pl.when(i == 0)
+        @pl.when(i == 2)
         def _():
             gather_last(0, 2)
             gather_last(0, 3)

time: 78.2 us -> 77.9 us (level)
  no operation moved by 1% of the time
where the time goes in v5:
time: 77.9 us; the launch traced here: 77.4 us
  Pallas kernels  75.6 us (97%)
  local copies, waits for them, and re-layouts  1.85 us (2%)
    pallas_call x1, Pallas kernels, body(): pl.pallas_call(kernel, name='attention_and_encoder', out_shape=jax.ShapeD...  75.6 us
    unnamed x1, local copies, waits for them, and re-layouts  1.85 us

profile of v5, /device:TPU:0, one launch (start us, length us, event | category | flops | bytes accessed | tf_op | source)
XLA Modules:
  0.0 77.4 jit_solution(14882459284808474304)
XLA Ops:
  0.0 75.6 %attention_and_encoder.1 = bf16[4,8,2,2048]{3,2,1,0:T(2,128)(2,1)} custom-call(bf16[4,8,4,2048]{3,2,1,0:T(4,128)(2,1)} %x_hbm.1, bf16[2048,2048]{1,0:T(8,128)(2,1)} %wh_hbm.1, bf16[2048,512]{1,0:T(8,128)(2,1)} %we_hbm.1, bf16[512,256]{1,0:T(8,128)(2,1)} %wq_hbm.1, bf16[512,256]{1,0:T(8,128)(2,1)} %wg_hbm.1, bf16[256,512]{1,0:T(8,128)(2,1)} %wp_hbm.1, ...), custom_call_target="tpu_custom_call" | custom-call | tf_op jit(solution)/shard_map/attention_and_encoder/pallas_call | solution.py:392
  75.6 1.8 %copy.12 = bf16[4,8,2,2048]{3,2,1,0:T(2,128)(2,1)} copy(bf16[4,8,2,2048]{3,2,1,0:T(2,128)(2,1)} %attention_and_encoder.1) | data formatting | bytes 524288

commit v6 on v5

--- a/solution.py
+++ b/solution.py
@@ -21,7 +21,7 @@
     [(a, b, c) for a in range(4) for b in range(4) for c in range(2) if a or b or c],
     key=lambda t: -(min(t[0], 4 - t[0]) + min(t[1], 4 - t[1]) + 2 * t[2]),
 )
-HID_CHUNKS = 4
+HID_CHUNKS = 2
 HID_CHUNK = HALF // HID_CHUNKS
 OUT_CHUNKS = 4
 OUT_CHUNK = WIDTH // OUT_CHUNKS

time: 77.9 us -> 76.9 us (0.987)
  Pallas kernels: 75.6 us -> 74.7 us
    pallas_call x1, Pallas kernels: 75.6 us -> 74.7 us  [body(): pl.pallas_call(kernel, name='attention_and_encoder', out_shape=jax.ShapeD...]
where the time goes in v6:
time: 76.9 us; the launch traced here: 76.6 us
  Pallas kernels  74.7 us (97%)
  local copies, waits for them, and re-layouts  1.85 us (2%)
    pallas_call x1, Pallas kernels, body(): pl.pallas_call(kernel, name='attention_and_encoder', out_shape=jax.ShapeD...  74.7 us
    unnamed x1, local copies, waits for them, and re-layouts  1.85 us

profile of v6, /device:TPU:0, one launch (start us, length us, event | category | flops | bytes accessed | tf_op | source)
XLA Modules:
  0.0 76.6 jit_solution(8827812508497505944)
XLA Ops:
  0.0 74.7 %attention_and_encoder.1 = bf16[4,8,2,2048]{3,2,1,0:T(2,128)(2,1)} custom-call(bf16[4,8,4,2048]{3,2,1,0:T(4,128)(2,1)} %x_hbm.1, bf16[2048,2048]{1,0:T(8,128)(2,1)} %wh_hbm.1, bf16[2048,512]{1,0:T(8,128)(2,1)} %we_hbm.1, bf16[512,256]{1,0:T(8,128)(2,1)} %wq_hbm.1, bf16[512,256]{1,0:T(8,128)(2,1)} %wg_hbm.1, bf16[256,512]{1,0:T(8,128)(2,1)} %wp_hbm.1, ...), custom_call_target="tpu_custom_call" | custom-call | tf_op jit(solution)/shard_map/attention_and_encoder/pallas_call | solution.py:392
  74.8 1.8 %copy.12 = bf16[4,8,2,2048]{3,2,1,0:T(2,128)(2,1)} copy(bf16[4,8,2,2048]{3,2,1,0:T(2,128)(2,1)} %attention_and_encoder.1) | data formatting | bytes 524288
